TPU v7x, 32 devices: a whole 2x2x4 slice. The times are simulated.
32 devices in a mesh: groups: 2 (over x), shard: 8 (over z, y), sub: 2 (over core).
Axes of the slice: x: 2, y: 2, z: 4, core: 2. Of those that a mesh axis runs over, the one named last changes fastest.
Arguments:
- queries: bfloat16 [256, 32, 128], P(('groups', 'shard', 'sub')), parts along dimension 0, may hold values from -0.19921875 to 0.19921875
- documents: bfloat16 [4096, 128, 128], P(('shard', 'sub')), may hold values from -0.59765625 to 0.59765625
- doc_lengths: int32 [4096], P(('shard', 'sub')), may hold values from 1 to 128
- candidates: int32 [256, 128], P('groups', ('shard', 'sub')), parts along dimension 0, may hold values from -1 to 255, as said below
Outputs:
- scores: float32 [256, 128], P(('groups', 'shard', 'sub')), parts along dimension 0
There are 2 independent parts, one for each index of `groups`. A program takes and returns all parts, laid end to end along the dimension named above; an argument that names none is the same for every part. Nothing has to cross between parts.
Inputs may be any that keep to these rules, and one draw needn't show every extreme that they name: `candidates`: -1 marks an empty slot; column c names a document block of device c // 8.
All inputs are finite; a program needn't handle non-finite values.
Results may differ from a plain program's by a relative error of at most 0.0003.
Values may be sent and summed in bfloat16 or wider, within the bound.
No kernel may reach another device: no remote copies, remote signals or barrier semaphores. Data moves between devices by JAX's collectives and lax.ppermute only.
A program may use at most 64 MiB of HBM per device.

v0:
```python
import jax
import jax.numpy as jnp
from jax import lax
from jax.sharding import PartitionSpec as P


def shards(queries, documents, doc_lengths, candidates):
    token_pos = jnp.arange(documents.shape[1], dtype=jnp.int32)
    usable_all = token_pos[None, :] < doc_lengths[:, None]

    def score_query(pair):
        one_query, slot_ids = pair
        filled = slot_ids >= 0
        doc_rows = jnp.maximum(slot_ids, 0)
        picked = documents[doc_rows]
        similar = jnp.einsum("td,skd->stk", one_query, picked, preferred_element_type=jnp.float32)
        usable = usable_all[doc_rows]
        top_match = jnp.max(jnp.where(usable[:, None, :], similar, -jnp.inf), axis=2)
        return jnp.where(filled, jnp.sum(top_match, axis=1), jnp.zeros((), jnp.float32))

    local_scores = lax.map(
        score_query,
        (lax.all_gather(queries, ("shard", "sub"), axis=0, tiled=True), candidates),
        batch_size=16,
    )
    devices = lax.axis_size(("shard", "sub"))
    position = lax.axis_index(("shard", "sub"))
    slot_count = local_scores.shape[1]
    spread = jnp.zeros((local_scores.shape[0], devices * slot_count), jnp.float32)
    spread = lax.dynamic_update_slice_in_dim(spread, local_scores, position * slot_count, 1)
    return lax.psum_scatter(spread, ("shard", "sub"), scatter_dimension=0, tiled=True)


def solution(mesh):
    in_specs = (
        P(("groups", "shard", "sub"), None, None),
        P(("shard", "sub"), None, None),
        P(("shard", "sub")),
        P("groups", ("shard", "sub")),
    )
    out_specs = P(("groups", "shard", "sub"), None)
    return jax.shard_map(shards, mesh=mesh, in_specs=in_specs, out_specs=out_specs, check_vma=False)
```

profile of v0, /device:TPU:0, one launch (start us, length us, event | category | flops | bytes accessed | tf_op | source)
XLA Modules:
  0.0 234.4 jit_solution(17033976865754134036)
XLA Ops:
  6.5 0.7 all-gather.2.cloned.1.call-update
  7.3 0.8 reshape.24
  8.1 42.1 %all-gather.2.cloned.1.call-done = bf16[128,32,128]{2,1,0:T(8,128)(2,1)} async-done(((bf16[8,32,128]{2,1,0:T(8,128)(2,1)}), bf16[128,32,128]{2,1,0:T(8,128)(2,1)}) %all-gather.2.cloned.1.call-update) | async-done | bytes 1048592 | tf_op jit(solution)/shard_map/all_gather | solution.py:23
  50.2 91.3 %while.11 = (s32[]{:T(128)}, f32[8,16,8]{1,2,0:T(8,128)S(1)}, s32[8,16,8]{1,0,2:T(8,128)S(1)}, bf16[256,128,128]{2,1,0:T(8,128)(2,1)}, bf16[8,16,32,128]{3,2,1,0...) while((s32[]{:T(128)}, f32[8,16,8]{1,2,0:T(8,128)S(1)}, s32[8,16,8]{1,0,2:T(8,128)S(1)}, ...), condition=%wide.region_3.4_spmd.clone, body=%wide.region_0.3_spmd.clone.sunk | while | flops 135300352 | bytes 12857981 | solution.py:21
  50.4 6.4 %gather_fusion = bf16[128,128,128]{2,1,0:T(8,128)(2,1)} fusion(bf16[256,128,128]{2,1,0:T(8,128)(2,1)} %get-tuple-element.139, s32[1024]{0:T(1024)S(1)} %pad_clamp_fusion.2), kind=kCustom, calls=%fused_computation.1.clone.clone.1 | custom fusion | bytes 8389120 | tf_op jit(solution)/shard_map/while/body/eval_jaxpr/vmap()/gather | solution.py:15
  56.8 0.1 iota_compare_fusion.2
  56.9 0.7 gather_fusion.1
  57.6 3.8 %select_reduce_fusion.2 = f32[16,8,32]{2,1,0:T(8,128)S(1)} fusion(bf16[16,8,128,128]{3,2,1,0:T(8,128)(2,1)} %bitcast.31, pred[16,8,128]{2,1,0:T(8,128)(4,1)S(1)} %bitcast.34, bf16[8,16,32,128]{3,2,1,0:T(8,128)(2,1)} %get-tuple-element.140, s32[]{:T(128)} %get-tuple-element.128), kind=kOutput, calls=%fused_computation.3.clone.1 | convolution fusion | flops 135262208 | bytes 4358656 | tf_op jit(solution)/shard_map/while/body/eval_jaxpr/vmap(td,skd->stk)/dot_general | solution.py:16
  61.4 0.1 reduce_sum.14
  61.8 6.4 %gather_fusion = bf16[128,128,128]{2,1,0:T(8,128)(2,1)} fusion(bf16[256,128,128]{2,1,0:T(8,128)(2,1)} %get-tuple-element.139, s32[1024]{0:T(1024)S(1)} %pad_clamp_fusion.2), kind=kCustom, calls=%fused_computation.1.clone.clone.1 | custom fusion | bytes 8389120 | tf_op jit(solution)/shard_map/while/body/eval_jaxpr/vmap()/gather | solution.py:15
  68.2 0.1 iota_compare_fusion.2
  68.3 0.7 gather_fusion.1
  69.0 3.8 %select_reduce_fusion.2 = f32[16,8,32]{2,1,0:T(8,128)S(1)} fusion(bf16[16,8,128,128]{3,2,1,0:T(8,128)(2,1)} %bitcast.31, pred[16,8,128]{2,1,0:T(8,128)(4,1)S(1)} %bitcast.34, bf16[8,16,32,128]{3,2,1,0:T(8,128)(2,1)} %get-tuple-element.140, s32[]{:T(128)} %get-tuple-element.128), kind=kOutput, calls=%fused_computation.3.clone.1 | convolution fusion | flops 135262208 | bytes 4358656 | tf_op jit(solution)/shard_map/while/body/eval_jaxpr/vmap(td,skd->stk)/dot_general | solution.py:16
  72.8 0.1 reduce_sum.14
  73.2 6.4 %gather_fusion = bf16[128,128,128]{2,1,0:T(8,128)(2,1)} fusion(bf16[256,128,128]{2,1,0:T(8,128)(2,1)} %get-tuple-element.139, s32[1024]{0:T(1024)S(1)} %pad_clamp_fusion.2), kind=kCustom, calls=%fused_computation.1.clone.clone.1 | custom fusion | bytes 8389120 | tf_op jit(solution)/shard_map/while/body/eval_jaxpr/vmap()/gather | solution.py:15
  79.6 0.1 iota_compare_fusion.2
  79.7 0.7 gather_fusion.1
  80.4 3.8 %select_reduce_fusion.2 = f32[16,8,32]{2,1,0:T(8,128)S(1)} fusion(bf16[16,8,128,128]{3,2,1,0:T(8,128)(2,1)} %bitcast.31, pred[16,8,128]{2,1,0:T(8,128)(4,1)S(1)} %bitcast.34, bf16[8,16,32,128]{3,2,1,0:T(8,128)(2,1)} %get-tuple-element.140, s32[]{:T(128)} %get-tuple-element.128), kind=kOutput, calls=%fused_computation.3.clone.1 | convolution fusion | flops 135262208 | bytes 4358656 | tf_op jit(solution)/shard_map/while/body/eval_jaxpr/vmap(td,skd->stk)/dot_general | solution.py:16
  84.2 0.1 reduce_sum.14
  84.6 6.4 %gather_fusion = bf16[128,128,128]{2,1,0:T(8,128)(2,1)} fusion(bf16[256,128,128]{2,1,0:T(8,128)(2,1)} %get-tuple-element.139, s32[1024]{0:T(1024)S(1)} %pad_clamp_fusion.2), kind=kCustom, calls=%fused_computation.1.clone.clone.1 | custom fusion | bytes 8389120 | tf_op jit(solution)/shard_map/while/body/eval_jaxpr/vmap()/gather | solution.py:15
  91.0 0.1 iota_compare_fusion.2
  91.1 0.7 gather_fusion.1
  91.8 3.8 %select_reduce_fusion.2 = f32[16,8,32]{2,1,0:T(8,128)S(1)} fusion(bf16[16,8,128,128]{3,2,1,0:T(8,128)(2,1)} %bitcast.31, pred[16,8,128]{2,1,0:T(8,128)(4,1)S(1)} %bitcast.34, bf16[8,16,32,128]{3,2,1,0:T(8,128)(2,1)} %get-tuple-element.140, s32[]{:T(128)} %get-tuple-element.128), kind=kOutput, calls=%fused_computation.3.clone.1 | convolution fusion | flops 135262208 | bytes 4358656 | tf_op jit(solution)/shard_map/while/body/eval_jaxpr/vmap(td,skd->stk)/dot_general | solution.py:16
  95.7 0.1 reduce_sum.14
  96.0 6.4 %gather_fusion = bf16[128,128,128]{2,1,0:T(8,128)(2,1)} fusion(bf16[256,128,128]{2,1,0:T(8,128)(2,1)} %get-tuple-element.139, s32[1024]{0:T(1024)S(1)} %pad_clamp_fusion.2), kind=kCustom, calls=%fused_computation.1.clone.clone.1 | custom fusion | bytes 8389120 | tf_op jit(solution)/shard_map/while/body/eval_jaxpr/vmap()/gather | solution.py:15
  102.4 0.1 iota_compare_fusion.2
  102.6 0.7 gather_fusion.1
  103.2 3.8 %select_reduce_fusion.2 = f32[16,8,32]{2,1,0:T(8,128)S(1)} fusion(bf16[16,8,128,128]{3,2,1,0:T(8,128)(2,1)} %bitcast.31, pred[16,8,128]{2,1,0:T(8,128)(4,1)S(1)} %bitcast.34, bf16[8,16,32,128]{3,2,1,0:T(8,128)(2,1)} %get-tuple-element.140, s32[]{:T(128)} %get-tuple-element.128), kind=kOutput, calls=%fused_computation.3.clone.1 | convolution fusion | flops 135262208 | bytes 4358656 | tf_op jit(solution)/shard_map/while/body/eval_jaxpr/vmap(td,skd->stk)/dot_general | solution.py:16
  107.1 0.1 reduce_sum.14
  107.5 6.4 %gather_fusion = bf16[128,128,128]{2,1,0:T(8,128)(2,1)} fusion(bf16[256,128,128]{2,1,0:T(8,128)(2,1)} %get-tuple-element.139, s32[1024]{0:T(1024)S(1)} %pad_clamp_fusion.2), kind=kCustom, calls=%fused_computation.1.clone.clone.1 | custom fusion | bytes 8389120 | tf_op jit(solution)/shard_map/while/body/eval_jaxpr/vmap()/gather | solution.py:15
  113.9 0.1 iota_compare_fusion.2
  114.0 0.7 gather_fusion.1
  114.7 3.8 %select_reduce_fusion.2 = f32[16,8,32]{2,1,0:T(8,128)S(1)} fusion(bf16[16,8,128,128]{3,2,1,0:T(8,128)(2,1)} %bitcast.31, pred[16,8,128]{2,1,0:T(8,128)(4,1)S(1)} %bitcast.34, bf16[8,16,32,128]{3,2,1,0:T(8,128)(2,1)} %get-tuple-element.140, s32[]{:T(128)} %get-tuple-element.128), kind=kOutput, calls=%fused_computation.3.clone.1 | convolution fusion | flops 135262208 | bytes 4358656 | tf_op jit(solution)/shard_map/while/body/eval_jaxpr/vmap(td,skd->stk)/dot_general | solution.py:16
  118.5 0.1 reduce_sum.14
  118.9 6.4 %gather_fusion = bf16[128,128,128]{2,1,0:T(8,128)(2,1)} fusion(bf16[256,128,128]{2,1,0:T(8,128)(2,1)} %get-tuple-element.139, s32[1024]{0:T(1024)S(1)} %pad_clamp_fusion.2), kind=kCustom, calls=%fused_computation.1.clone.clone.1 | custom fusion | bytes 8389120 | tf_op jit(solution)/shard_map/while/body/eval_jaxpr/vmap()/gather | solution.py:15
  125.3 0.1 iota_compare_fusion.2
  125.4 0.7 gather_fusion.1
  126.1 3.8 %select_reduce_fusion.2 = f32[16,8,32]{2,1,0:T(8,128)S(1)} fusion(bf16[16,8,128,128]{3,2,1,0:T(8,128)(2,1)} %bitcast.31, pred[16,8,128]{2,1,0:T(8,128)(4,1)S(1)} %bitcast.34, bf16[8,16,32,128]{3,2,1,0:T(8,128)(2,1)} %get-tuple-element.140, s32[]{:T(128)} %get-tuple-element.128), kind=kOutput, calls=%fused_computation.3.clone.1 | convolution fusion | flops 135262208 | bytes 4358656 | tf_op jit(solution)/shard_map/while/body/eval_jaxpr/vmap(td,skd->stk)/dot_general | solution.py:16
  130.3 6.4 %gather_fusion = bf16[128,128,128]{2,1,0:T(8,128)(2,1)} fusion(bf16[256,128,128]{2,1,0:T(8,128)(2,1)} %get-tuple-element.139, s32[1024]{0:T(1024)S(1)} %pad_clamp_fusion.2), kind=kCustom, calls=%fused_computation.1.clone.clone.1 | custom fusion | bytes 8389120 | tf_op jit(solution)/shard_map/while/body/eval_jaxpr/vmap()/gather | solution.py:15
  136.7 0.1 iota_compare_fusion.2
  136.8 0.7 gather_fusion.1
  137.5 3.8 %select_reduce_fusion.2 = f32[16,8,32]{2,1,0:T(8,128)S(1)} fusion(bf16[16,8,128,128]{3,2,1,0:T(8,128)(2,1)} %bitcast.31, pred[16,8,128]{2,1,0:T(8,128)(4,1)S(1)} %bitcast.34, bf16[8,16,32,128]{3,2,1,0:T(8,128)(2,1)} %get-tuple-element.140, s32[]{:T(128)} %get-tuple-element.128), kind=kOutput, calls=%fused_computation.3.clone.1 | convolution fusion | flops 135262208 | bytes 4358656 | tf_op jit(solution)/shard_map/while/body/eval_jaxpr/vmap(td,skd->stk)/dot_general | solution.py:16
  141.3 0.1 reduce_sum.14
  141.6 0.4 dynamic_update_slice.7
  142.0 0.6 copy-done
  142.6 0.6 dynamic-slice
  143.9 82.5 %all-reduce.3.cloned.1.call-done = f32[128,128]{1,0:T(8,128)} async-done(((f32[128,128]{1,0:T(8,128)}), f32[128,128]{1,0:T(8,128)}) %all-reduce.3.cloned.1.call-update) | async-done | bytes 65552
  226.3 1.3 constant_dynamic-slice_fusion.1
  (82 shorter events, 2.3 us)
Async XLA Ops:
  6.5 43.7 %all-gather.2.cloned.1.call-start = ((), (), s32[]{:S(2)}) async-start(), calls=%async_computation | async-start | bytes 1114112 | tf_op jit(solution)/shard_map/all_gather | solution.py:23
  7.3 219.1 %all-reduce.3.cloned.1.call-start = ((), (), s32[]{:S(2)}) async-start(), calls=%async_computation.1 | async-start | bytes 131072
  50.2 92.4 %copy-start.2 = (u32[32]{0:T(128)S(1)}, u32[32]{0:T(128)}, u32[]{:S(2)}) copy-start(u32[32]{0:T(128)} %constant.41) | copy-start | bytes 388
  50.4 6.4 %copy-start.1 = (s32[256]{0:T(256)S(1)}, s32[256]{0:T(256)}, u32[]{:S(2)}) copy-start(s32[256]{0:T(256)} %get-tuple-element.141) | copy-start | bytes 3076 | tf_op jit(solution)/shard_map/while
  61.8 6.4 %copy-start.1 = (s32[256]{0:T(256)S(1)}, s32[256]{0:T(256)}, u32[]{:S(2)}) copy-start(s32[256]{0:T(256)} %get-tuple-element.141) | copy-start | bytes 3076 | tf_op jit(solution)/shard_map/while
  73.2 6.4 %copy-start.1 = (s32[256]{0:T(256)S(1)}, s32[256]{0:T(256)}, u32[]{:S(2)}) copy-start(s32[256]{0:T(256)} %get-tuple-element.141) | copy-start | bytes 3076 | tf_op jit(solution)/shard_map/while
  84.6 6.4 %copy-start.1 = (s32[256]{0:T(256)S(1)}, s32[256]{0:T(256)}, u32[]{:S(2)}) copy-start(s32[256]{0:T(256)} %get-tuple-element.141) | copy-start | bytes 3076 | tf_op jit(solution)/shard_map/while
  96.0 6.4 %copy-start.1 = (s32[256]{0:T(256)S(1)}, s32[256]{0:T(256)}, u32[]{:S(2)}) copy-start(s32[256]{0:T(256)} %get-tuple-element.141) | copy-start | bytes 3076 | tf_op jit(solution)/shard_map/while
  107.4 6.4 %copy-start.1 = (s32[256]{0:T(256)S(1)}, s32[256]{0:T(256)}, u32[]{:S(2)}) copy-start(s32[256]{0:T(256)} %get-tuple-element.141) | copy-start | bytes 3076 | tf_op jit(solution)/shard_map/while
  118.9 6.4 %copy-start.1 = (s32[256]{0:T(256)S(1)}, s32[256]{0:T(256)}, u32[]{:S(2)}) copy-start(s32[256]{0:T(256)} %get-tuple-element.141) | copy-start | bytes 3076 | tf_op jit(solution)/shard_map/while
  130.3 6.4 %copy-start.1 = (s32[256]{0:T(256)S(1)}, s32[256]{0:T(256)}, u32[]{:S(2)}) copy-start(s32[256]{0:T(256)} %get-tuple-element.141) | copy-start | bytes 3076 | tf_op jit(solution)/shard_map/while
  142.0 0.6 copy-start
Sparse Core Ops, SparseCore 0:
  9.5 40.6 all-gather.1
  142.7 83.5 all-reduce.2
where the time goes:
time: 236 us; the launch traced here: 234 us
  waiting for transfers between devices  125 us (53%)
  local copies, waits for them, and re-layouts  62.4 us (26%)
  matrix products  30.5 us (13%)
  between operations  14.1 us (6%)
    unnamed x3, waiting for transfers between devices  83.2 us
    gather x8, local copies, waits for them, and re-layouts, score_query(): picked = documents[doc_rows]  51.2 us
    all_gather x1, waiting for transfers between devices, shards(): lax.all_gather(queries, ('shard', 'sub'), axis=0, tiled=True)  42.1 us
    dot_general x8, matrix products, score_query(): jnp.einsum('td,skd->stk', one_query, picked, preferred_element_type=jnp.f...  30.5 us
    gather x8, local copies, waits for them, and re-layouts, score_query(): usable = usable_all[doc_rows]  5.5 us
  transfers between devices with their start and end apart: 2, of which 2 were waited for; matrix products, arithmetic and copies ran while one was open for 1% of the time, Pallas kernels for 0%

commit v1 on v0

v1 whole, which is shorter than its diff:
```python
import functools

import jax
import jax.numpy as jnp
from jax import lax
from jax.experimental import pallas as pl
from jax.experimental.pallas import tpu as pltpu
from jax.sharding import PartitionSpec as P

AXES = ("shard", "sub")
VMEM = pl.BlockSpec(memory_space=pltpu.VMEM)
SMEM = pl.BlockSpec(memory_space=pltpu.SMEM)


def prepare_kernel(lengths, documents, out):
    count, tokens, dim = documents.shape
    step = pl.program_id(0)
    row = lax.broadcasted_iota(jnp.int32, (tokens, dim), 0)

    @pl.when(step < pl.num_programs(0) - 1)
    def _():
        def body(i, carry):
            block = documents[i]
            out[i] = jnp.where(row < lengths[step * count + i], block, block[0:1, :])
            return carry

        lax.fori_loop(0, count, body, 0, unroll=4)

    @pl.when(step == pl.num_programs(0) - 1)
    def _():
        out[...] = jnp.zeros(out.shape, out.dtype)


def prepare(lengths, documents):
    count, tokens, dim = documents.shape
    part = 32
    steps = count // part
    size = documents.size * 2
    return pl.pallas_call(
        prepare_kernel,
        grid=(steps + 1,),
        out_shape=jax.ShapeDtypeStruct((count + part, tokens, dim), documents.dtype),
        in_specs=[SMEM, pl.BlockSpec((part, tokens, dim), lambda i: (jnp.minimum(i, steps - 1), 0, 0))],
        out_specs=pl.BlockSpec((part, tokens, dim), lambda i: (i, 0, 0)),
        compiler_params=pltpu.CompilerParams(vmem_limit_bytes=48 << 20),
        cost_estimate=pl.CostEstimate(flops=documents.size * 10, bytes_accessed=2 * size, transcendentals=0),
        name="prepare",
    )(lengths, documents)


def score_kernel(shifts, n_blocks, candidates, *refs):
    blocks, documents, outs, held = refs[:n_blocks], refs[n_blocks], refs[n_blocks + 1 : -1], refs[-1]
    me = lax.axis_index("shard") * lax.axis_size("sub") + lax.axis_index("sub")
    slots = candidates.shape[0]
    empty = documents.shape[0] - 1
    n_queries, terms, dim = blocks[0].shape
    half = slots // 2
    width = outs[0].shape[-1]
    tokens = documents.shape[1]
    for b, block in enumerate(blocks):
        held[pl.ds(b * n_queries, n_queries)] = block[...]
    lane = lax.broadcasted_iota(jnp.int32, (slots, width), 1)
    pair = lax.broadcasted_iota(jnp.int32, (slots, width), 0) % half
    at_first = lane == me * slots + pair
    at_second = lane == me * slots + half + pair
    first = lax.broadcasted_iota(jnp.int32, (slots, 2 * terms), 1) < terms
    nothing = jnp.zeros((terms, dim), documents.dtype)

    def tops(place, column):
        query = held[place]
        both = jnp.concatenate(
            [jnp.concatenate([query, nothing], 1), jnp.concatenate([nothing, query], 1)], 0
        )
        rows = []
        for s in range(slots):
            named = candidates[s, column]
            rows.append(jnp.where(named >= 0, named, empty))
        found = []
        for p in range(half):
            sides = jnp.concatenate([documents[rows[p]], documents[rows[p + half]]], 1)
            similar = lax.dot_general(
                sides, both, (((1,), (1,)), ((), ())), preferred_element_type=jnp.float32
            )
            found.append(jnp.max(similar, axis=0, keepdims=True))
        return found

    def block_scores(b, out, o):
        owner = me ^ shifts[b]
        for i in range(0, n_queries, 2):
            top = jnp.concatenate(
                tops(b * n_queries + i, owner * n_queries + i)
                + tops(b * n_queries + i + 1, owner * n_queries + i + 1),
                0,
            )
            one = jnp.sum(jnp.where(first, top, 0.0), axis=1, keepdims=True)
            two = jnp.sum(jnp.where(first, 0.0, top), axis=1, keepdims=True)
            spread = jnp.where(at_first, one, jnp.where(at_second, two, 0.0))
            out[o, i : i + 1, :] = jnp.sum(spread[:half], axis=0, keepdims=True)
            out[o, i + 1 : i + 2, :] = jnp.sum(spread[half:], axis=0, keepdims=True)

    for b in range(n_blocks):
        block_scores(b, outs[b // 2], b % 2)


def score(shifts, candidates, blocks, documents, width):
    n_blocks = len(blocks)
    n_queries, terms, dim = blocks[0].shape
    tokens = documents.shape[1]
    pairs = n_blocks * n_queries * candidates.shape[0]
    flops = 2 * pairs * terms * dim * tokens * 8
    return pl.pallas_call(
        functools.partial(score_kernel, shifts, n_blocks),
        out_shape=[jax.ShapeDtypeStruct((2, n_queries, width), jnp.float32)] * (n_blocks // 2),
        in_specs=[SMEM] + [VMEM] * (n_blocks + 1),
        out_specs=[VMEM] * (n_blocks // 2),
        scratch_shapes=[pltpu.VMEM((n_blocks * n_queries, terms, dim), blocks[0].dtype)],
        compiler_params=pltpu.CompilerParams(vmem_limit_bytes=16 << 20),
        cost_estimate=pl.CostEstimate(flops=flops, bytes_accessed=0, transcendentals=0),
        name="score",
    )(candidates, *blocks, documents)


def shards(queries, documents, doc_lengths, candidates):
    shard, sub = lax.axis_size("shard"), lax.axis_size("sub")
    devices = shard * sub

    def swap(value, k):
        return lax.ppermute(value, AXES, [(i, i ^ k) for i in range(devices)])

    width = devices * candidates.shape[1]
    columns = candidates.T
    steps = [z * 4 for z in range(shard // 2)]
    along = {z: (queries if z == 0 else swap(queries, z)) for z in reversed(steps)}
    ready = prepare(doc_lengths, documents)
    across = {z: swap(along[z], 2) for z in reversed(steps)}
    near_sum, far_sum = [], []
    for z in reversed(steps):
        blocks = [along[z], swap(along[z], 1), across[z], swap(across[z], 1)]
        near, far = score((z, z ^ 1, z ^ 2, z ^ 3), columns, blocks, ready, width)
        near_sum.append(near if z == 0 else swap(near, z))
        far_sum.append(far if z == 0 else swap(far, z))
    mine = sum(near_sum[1:], near_sum[0]) + swap(sum(far_sum[1:], far_sum[0]), 2)
    return mine[0] + swap(mine[1], 1)


def solution(mesh):
    in_specs = (
        P(("groups", "shard", "sub"), None, None),
        P(("shard", "sub"), None, None),
        P(("shard", "sub")),
        P("groups", ("shard", "sub")),
    )
    out_specs = P(("groups", "shard", "sub"), None)
    return jax.shard_map(shards, mesh=mesh, in_specs=in_specs, out_specs=out_specs, check_vma=False)
```

time: 236 us -> 58.6 us (0.25)
  waiting for transfers between devices: 125 us -> 6.42 us
  local copies, waits for them, and re-layouts: 62.4 us -> 4.36 us
  matrix products: 30.5 us -> 0 us
  starting transfers between devices: 0.04 us -> 23.9 us
  Pallas kernels: 0 us -> 22.9 us
  between operations: 14.1 us -> 0.06 us
    unnamed x3 -> x0, waiting for transfers between devices: 83.2 us -> none
    gather x16 -> x0, local copies, waits for them, and re-layouts: 56.7 us -> none  [the longest x8 51.2 us: score_query(): picked = documents[doc_rows]]
    all_gather x1 -> x0, waiting for transfers between devices: 42.1 us -> none  [shards(): lax.all_gather(queries, ('shard', 'sub'), axis=0, tiled=True)]
    dot_general x8 -> x0, matrix products: 30.5 us -> none  [score_query(): jnp.einsum('td,skd->stk', one_query, picked, preferred_element_type=jnp.f...]
    ppermute x0 -> x23, starting transfers between devices: none -> 23.9 us  [swap(): return lax.ppermute(value, AXES, [(i, i ^ k) for i in range(devices)])]
    pallas_call x0 -> x5, Pallas kernels: none -> 22.9 us  [the longest x4 12.1 us: score(): pl.pallas_call(functools.partial(score_kernel, shifts, n_blocks), out_sha...]
    ppermute x0 -> x23, waiting for transfers between devices: none -> 6.42 us  [swap(): return lax.ppermute(value, AXES, [(i, i ^ k) for i in range(devices)])]
  transfers between devices with their start and end apart: 2 -> 23, of which waited for: 2 -> 4; matrix products, arithmetic and copies ran while one was open for 1% -> 0% of each run, Pallas kernels for 0% -> 39%
where the time goes in v1:
time: 58.6 us; the launch traced here: 58.2 us
  starting transfers between devices  23.9 us (41%)
  Pallas kernels  22.9 us (39%)
  waiting for transfers between devices  6.42 us (11%)
  local copies, waits for them, and re-layouts  4.36 us (7%)
  other arithmetic  0.61 us (1%)
    ppermute x23, starting transfers between devices, swap(): return lax.ppermute(value, AXES, [(i, i ^ k) for i in range(devices)])  23.9 us
    pallas_call x4, Pallas kernels, score(): pl.pallas_call(functools.partial(score_kernel, shifts, n_blocks), out_sha...  12.1 us
    pallas_call x1, Pallas kernels, prepare(): pl.pallas_call(prepare_kernel, grid=(steps + 1,), out_shape=jax.ShapeDtyp...  10.7 us
    ppermute x23, waiting for transfers between devices, swap(): return lax.ppermute(value, AXES, [(i, i ^ k) for i in range(devices)])  6.42 us
    unnamed x8, local copies, waits for them, and re-layouts  4.36 us
  transfers between devices with their start and end apart: 23, of which 4 were waited for; matrix products, arithmetic and copies ran while one was open for 0% of the time, Pallas kernels for 39%

profile of v1, /device:TPU:0, one launch (start us, length us, event | category | flops | bytes accessed | tf_op | source)
XLA Modules:
  0.0 58.2 jit_solution(10719812740953368775)
XLA Ops:
  0.0 5.0 %collective-permute-start = (bf16[8,32,128]{2,1,0:T(8,128)(2,1)}, bf16[8,32,128]{2,1,0:T(8,128)(2,1)S(1)}, u32[]{:S(2)}, u32[]{:S(2)}) collective-permute-start(bf16[8,32,128]{2,1,0:T(8,128)(2,1)} %refs_0_.1), channel_id=1, source_target_pairs={{0,12},{1,13},{2,14},{3,15},{4,8},{5,9},{6,10},{7,11},{8,4},{9,5},... | collective-permute-start | bytes 196616 | tf_op jit(solution)/shard_map/ppermute | solution.py:128
  5.1 0.0 collective-permute-start.5
  5.1 2.9 %collective-permute-done.refs_0_ = bf16[8,32,128]{2,1,0:T(8,128)(2,1)S(1)} collective-permute-done((bf16[8,32,128]{2,1,0:T(8,128)(2,1)}, bf16[8,32,128]{2,1,0:T(8,128)(2,1)S(1)}, u32[]{:S(2)}, u32[]{:S(2)}) %collective-permute-start) | collective-permute-done | bytes 65568 | tf_op jit(solution)/shard_map/ppermute | solution.py:128
  8.0 1.7 %collective-permute-start.2 = (bf16[8,32,128]{2,1,0:T(8,128)(2,1)S(1)}, bf16[8,32,128]{2,1,0:T(8,128)(2,1)S(1)}, u32[]{:S(2)}, u32[]{:S(2)}) collective-permute-start(bf16[8,32,128]{2,1,0:T(8,128)(2,1)S(1)} %collective-permute-done.refs_0_), channel_id=1, source_target_pairs={{0,2},{1,3},{2,0},{3,1},{4,6},{5,7},{6,4},{7,5},{8,10},{9,11},{10,... | collective-permute-start | bytes 196616 | tf_op jit(solution)/shard_map/ppermute | solution.py:128
  9.7 2.2 %collective-permute-start.10 = (bf16[8,32,128]{2,1,0:T(8,128)(2,1)}, bf16[8,32,128]{2,1,0:T(8,128)(2,1)S(1)}, u32[]{:S(2)}, u32[]{:S(2)}) collective-permute-start(bf16[8,32,128]{2,1,0:T(8,128)(2,1)} %refs_0_.1), channel_id=1, source_target_pairs={{0,4},{1,5},{2,6},{3,7},{4,0},{5,1},{6,2},{7,3},{8,12},{9,13},{10,... | collective-permute-start | bytes 196616 | tf_op jit(solution)/shard_map/ppermute | solution.py:128
  11.9 0.0 collective-permute-start.1
  11.9 0.0 collective-permute-done.5.refs_0_
  11.9 0.7 %collective-permute-start.7 = (bf16[8,32,128]{2,1,0:T(8,128)(2,1)S(1)}, bf16[8,32,128]{2,1,0:T(8,128)(2,1)S(1)}, u32[]{:S(2)}, u32[]{:S(2)}) collective-permute-start(bf16[8,32,128]{2,1,0:T(8,128)(2,1)S(1)} %collective-permute-done.5.refs_0_), channel_id=1, source_target_pairs={{0,2},{1,3},{2,0},{3,1},{4,6},{5,7},{6,4},{7,5},{8,10},{9,11},{10,... | collective-permute-start | bytes 196616 | tf_op jit(solution)/shard_map/ppermute | solution.py:128
  12.6 0.0 collective-permute-done.2.refs_2_
  12.6 0.2 collective-permute-start.3
  12.9 1.3 %collective-permute-start.16 = (bf16[8,32,128]{2,1,0:T(8,128)(2,1)}, bf16[8,32,128]{2,1,0:T(8,128)(2,1)S(1)}, u32[]{:S(2)}, u32[]{:S(2)}) collective-permute-start(bf16[8,32,128]{2,1,0:T(8,128)(2,1)} %refs_0_.1), channel_id=1, source_target_pairs={{0,2},{1,3},{2,0},{3,1},{4,6},{5,7},{6,4},{7,5},{8,10},{9,11},{10,... | collective-permute-start | bytes 196616 | tf_op jit(solution)/shard_map/ppermute | solution.py:128
  14.2 0.7 %copy-done.3 = s32[256]{0:T(256)S(1)} copy-done((s32[256]{0:T(256)S(1)}, s32[256]{0:T(256)}, u32[]{:S(2)}) %copy-start.3) | copy-done | bytes 1048
  14.8 10.7 %prepare.1.refs_4_ = bf16[288,128,128]{2,1,0:T(8,128)(2,1)} custom-call(s32[256]{0:T(256)S(1)} %copy-done.3, bf16[256,128,128]{2,1,0:T(8,128)(2,1)} %documents.1), custom_call_target="tpu_custom_call" | custom-call | flops 41943040 | bytes 16777216 | tf_op jit(solution)/shard_map/prepare/pallas_call | solution.py:39
  25.6 0.0 collective-permute-done.10.refs_0_
  25.6 0.1 collective-permute-start.15
  25.7 0.0 collective-permute-done.1.refs_1_
  25.7 0.5 collective-permute-start.6
  26.2 0.7 %collective-permute-start.12 = (bf16[8,32,128]{2,1,0:T(8,128)(2,1)S(1)}, bf16[8,32,128]{2,1,0:T(8,128)(2,1)S(1)}, u32[]{:S(2)}, u32[]{:S(2)}) collective-permute-start(bf16[8,32,128]{2,1,0:T(8,128)(2,1)S(1)} %collective-permute-done.10.refs_0_), channel_id=1, source_target_pairs={{0,2},{1,3},{2,0},{3,1},{4,6},{5,7},{6,4},{7,5},{8,10},{9,11},{10,... | collective-permute-start | bytes 196616 | tf_op jit(solution)/shard_map/ppermute | solution.py:128
  26.9 3.7 %copy-done = bf16[288,128,128]{2,1,0:T(8,128)(2,1)S(1)} copy-done((bf16[288,128,128]{2,1,0:T(8,128)(2,1)S(1)}, bf16[288,128,128]{2,1,0:T(8,128)(2,1)}, u32[]{:S(2)}) %copy-start) | copy-done | bytes 9437208
  30.6 3.0 %score.4 = (f32[2,8,128]{2,1,0:T(8,128)S(1)}, f32[2,8,128]{2,1,0:T(8,128)S(1)}) custom-call(s32[8,128]{1,0:T(8,128)S(1)} %bitcast.7, bf16[8,32,128]{2,1,0:T(8,128)(2,1)S(1)} %collective-permute-done.refs_0_, bf16[8,32,128]{2,1,0:T(8,128)(2,1)S(1)} %collective-permute-done.1.refs_1_, bf16[8,32,128]{2,1,0:T(8,128)(2,1)S(1)} %collective-permute-done.2.refs_2_, ...), custom_call_target="tpu_custom_call" | custom-call | flops 2147483648 | tf_op jit(solution)/shard_map/score/pallas_call | solution.py:111
  33.6 0.6 collective-permute-start.11
  34.2 0.0 collective-permute-done.6.refs_1_
  34.2 0.1 collective-permute-start.17
  34.3 0.0 collective-permute-done.12.refs_2_
  34.3 0.4 collective-permute-start.13
  34.7 0.0 collective-permute-done.8.refs_3_
  34.7 3.1 %collective-permute-start.18 = (f32[2,8,128]{2,1,0:T(8,128)S(1)}, f32[2,8,128]{2,1,0:T(8,128)S(1)}, u32[]{:S(2)}, u32[]{:S(2)}) collective-permute-start(f32[2,8,128]{2,1,0:T(8,128)S(1)} %get-tuple-element.17), channel_id=1, source_target_pairs={{0,12},{1,13},{2,14},{3,15},{4,8},{5,9},{6,10},{7,11},{8,4},{9,5},... | collective-permute-start | bytes 24584 | tf_op jit(solution)/shard_map/ppermute | solution.py:128
  37.8 3.0 %score.5 = (f32[2,8,128]{2,1,0:T(8,128)S(1)}, f32[2,8,128]{2,1,0:T(8,128)S(1)}) custom-call(s32[8,128]{1,0:T(8,128)S(1)} %bitcast.8, bf16[8,32,128]{2,1,0:T(8,128)(2,1)S(1)} %collective-permute-done.5.refs_0_, bf16[8,32,128]{2,1,0:T(8,128)(2,1)S(1)} %collective-permute-done.6.refs_1_, bf16[8,32,128]{2,1,0:T(8,128)(2,1)S(1)} %collective-permute-done.7.refs_2_, ...), custom_call_target="tpu_custom_call" | custom-call | flops 2147483648 | tf_op jit(solution)/shard_map/score/pallas_call | solution.py:111
  40.8 0.0 collective-permute-done.11.refs_1_
  40.9 0.4 collective-permute-start.19
  41.3 3.0 %score.6 = (f32[2,8,128]{2,1,0:T(8,128)S(1)}, f32[2,8,128]{2,1,0:T(8,128)S(1)}) custom-call(s32[8,128]{1,0:T(8,128)S(1)} %bitcast.9, bf16[8,32,128]{2,1,0:T(8,128)(2,1)S(1)} %collective-permute-done.10.refs_0_, bf16[8,32,128]{2,1,0:T(8,128)(2,1)S(1)} %collective-permute-done.11.refs_1_, bf16[8,32,128]{2,1,0:T(8,128)(2,1)S(1)} %collective-permute-done.12.refs_2_, ...), custom_call_target="tpu_custom_call" | custom-call | flops 2147483648 | tf_op jit(solution)/shard_map/score/pallas_call | solution.py:111
  44.3 0.9 %collective-permute-start.20 = (f32[2,8,128]{2,1,0:T(8,128)S(1)}, f32[2,8,128]{2,1,0:T(8,128)S(1)}, u32[]{:S(2)}, u32[]{:S(2)}) collective-permute-start(f32[2,8,128]{2,1,0:T(8,128)S(1)} %get-tuple-element.19), channel_id=1, source_target_pairs={{0,4},{1,5},{2,6},{3,7},{4,0},{5,1},{6,2},{7,3},{8,12},{9,13},{10,... | collective-permute-start | bytes 24584 | tf_op jit(solution)/shard_map/ppermute | solution.py:128
  45.2 0.0 collective-permute-done.15.refs_1_
  45.2 0.0 collective-permute-done.17.refs_3_
  45.3 3.0 %score.7 = (f32[2,8,128]{2,1,0:T(8,128)S(1)}, f32[2,8,128]{2,1,0:T(8,128)S(1)}) custom-call(s32[8,128]{1,0:T(8,128)S(1)} %bitcast.10, bf16[8,32,128]{2,1,0:T(8,128)(2,1)S(1)} %copy-done.1, bf16[8,32,128]{2,1,0:T(8,128)(2,1)S(1)} %collective-permute-done.15.refs_1_, bf16[8,32,128]{2,1,0:T(8,128)(2,1)S(1)} %collective-permute-done.16.refs_2_, ...), custom_call_target="tpu_custom_call" | custom-call | flops 2147483648 | tf_op jit(solution)/shard_map/score/pallas_call | solution.py:111
  48.3 3.1 %collective-permute-start.4 = (f32[2,8,128]{2,1,0:T(8,128)S(1)}, f32[2,8,128]{2,1,0:T(8,128)S(1)}, u32[]{:S(2)}, u32[]{:S(2)}) collective-permute-start(f32[2,8,128]{2,1,0:T(8,128)S(1)} %get-tuple-element.13), channel_id=1, source_target_pairs={{0,12},{1,13},{2,14},{3,15},{4,8},{5,9},{6,10},{7,11},{8,4},{9,5},... | collective-permute-start | bytes 24584 | tf_op jit(solution)/shard_map/ppermute | solution.py:128
  51.4 0.0 collective-permute-start.9
  51.4 0.0 collective-permute-done.18
  51.4 1.3 %collective-permute-start.14 = (f32[2,8,128]{2,1,0:T(8,128)S(1)}, f32[2,8,128]{2,1,0:T(8,128)S(1)}, u32[]{:S(2)}, u32[]{:S(2)}) collective-permute-start(f32[2,8,128]{2,1,0:T(8,128)S(1)} %get-tuple-element.15), channel_id=1, source_target_pairs={{0,4},{1,5},{2,6},{3,7},{4,0},{5,1},{6,2},{7,3},{8,12},{9,13},{10,... | collective-permute-start | bytes 24584 | tf_op jit(solution)/shard_map/ppermute | solution.py:128
  52.7 0.0 collective-permute-done.19
  52.7 0.0 collective-permute-done.20
  52.7 1.4 %collective-permute-start.21 = (f32[2,8,128]{2,1,0:T(8,128)S(1)}, f32[2,8,128]{2,1,0:T(8,128)S(1)}, u32[]{:S(2)}, u32[]{:S(2)}) collective-permute-start(f32[2,8,128]{2,1,0:T(8,128)S(1)} %add_add_fusion), channel_id=1, source_target_pairs={{0,2},{1,3},{2,0},{3,1},{4,6},{5,7},{6,4},{7,5},{8,10},{9,11},{10,... | collective-permute-start | bytes 24584 | tf_op jit(solution)/shard_map/ppermute | solution.py:128
  54.1 0.0 collective-permute-done.4
  54.1 1.8 %collective-permute-done.9 = f32[2,8,128]{2,1,0:T(8,128)S(1)} collective-permute-done((f32[2,8,128]{2,1,0:T(8,128)S(1)}, f32[2,8,128]{2,1,0:T(8,128)S(1)}, u32[]{:S(2)}, u32[]{:S(2)}) %collective-permute-start.9) | collective-permute-done | bytes 8224 | tf_op jit(solution)/shard_map/ppermute | solution.py:128
  56.0 0.5 collective-permute-done.21
  56.4 0.1 collective-permute-start.22
  56.5 1.2 %collective-permute-done.22 = f32[8,128]{1,0:T(8,128)S(1)} collective-permute-done((f32[8,128]{1,0:T(8,128)S(1)}, f32[8,128]{1,0:T(8,128)S(1)}, u32[]{:S(2)}, u32[]{:S(2)}) %collective-permute-start.22) | collective-permute-done | bytes 4128 | tf_op jit(solution)/shard_map/ppermute | solution.py:128
  57.7 0.6 %fusion = f32[8,128]{1,0:T(8,128)} fusion(f32[8,128]{1,0:T(8,128)S(1)} %collective-permute-done.22, f32[2,8,128]{2,1,0:T(8,128)S(1)} %add_add_fusion.1), kind=kLoop, calls=%fused_computation.4 | loop fusion | flops 1024 | bytes 12288 | tf_op jit(solution)/shard_map/add | solution.py:143
  (15 shorter events, 0.0 us)
Async XLA Ops:
  0.0 25.6 %copy-start.1 = (bf16[8,32,128]{2,1,0:T(8,128)(2,1)S(1)}, bf16[8,32,128]{2,1,0:T(8,128)(2,1)}, u32[]{:S(2)}) copy-start(bf16[8,32,128]{2,1,0:T(8,128)(2,1)} %refs_0_.1) | copy-start | bytes 196612
  0.0 26.9 %copy-start.2 = (s32[128,8]{0,1:T(8,128)S(1)}, s32[128,8]{0,1:T(8,128)}, u32[]{:S(2)}) copy-start(s32[128,8]{0,1:T(8,128)} %param.7) | copy-start | bytes 12292
  0.0 8.0 %collective-permute-start = (bf16[8,32,128]{2,1,0:T(8,128)(2,1)}, bf16[8,32,128]{2,1,0:T(8,128)(2,1)S(1)}, u32[]{:S(2)}, u32[]{:S(2)}) collective-permute-start(bf16[8,32,128]{2,1,0:T(8,128)(2,1)} %refs_0_.1), channel_id=1, source_target_pairs={{0,12},{1,13},{2,14},{3,15},{4,8},{5,9},{6,10},{7,11},{8,4},{9,5},... | collective-permute-start | bytes 196616 | tf_op jit(solution)/shard_map/ppermute | solution.py:128
  5.1 6.8 %collective-permute-start.5 = (bf16[8,32,128]{2,1,0:T(8,128)(2,1)}, bf16[8,32,128]{2,1,0:T(8,128)(2,1)S(1)}, u32[]{:S(2)}, u32[]{:S(2)}) collective-permute-start(bf16[8,32,128]{2,1,0:T(8,128)(2,1)} %refs_0_.1), channel_id=1, source_target_pairs={{0,8},{1,9},{2,10},{3,11},{4,12},{5,13},{6,14},{7,15},{8,0},{9,1},... | collective-permute-start | bytes 196616 | tf_op jit(solution)/shard_map/ppermute | solution.py:128
  8.0 4.6 %collective-permute-start.2 = (bf16[8,32,128]{2,1,0:T(8,128)(2,1)S(1)}, bf16[8,32,128]{2,1,0:T(8,128)(2,1)S(1)}, u32[]{:S(2)}, u32[]{:S(2)}) collective-permute-start(bf16[8,32,128]{2,1,0:T(8,128)(2,1)S(1)} %collective-permute-done.refs_0_), channel_id=1, source_target_pairs={{0,2},{1,3},{2,0},{3,1},{4,6},{5,7},{6,4},{7,5},{8,10},{9,11},{10,... | collective-permute-start | bytes 196616 | tf_op jit(solution)/shard_map/ppermute | solution.py:128
  9.7 15.9 %collective-permute-start.10 = (bf16[8,32,128]{2,1,0:T(8,128)(2,1)}, bf16[8,32,128]{2,1,0:T(8,128)(2,1)S(1)}, u32[]{:S(2)}, u32[]{:S(2)}) collective-permute-start(bf16[8,32,128]{2,1,0:T(8,128)(2,1)} %refs_0_.1), channel_id=1, source_target_pairs={{0,4},{1,5},{2,6},{3,7},{4,0},{5,1},{6,2},{7,3},{8,12},{9,13},{10,... | collective-permute-start | bytes 196616 | tf_op jit(solution)/shard_map/ppermute | solution.py:128
  11.9 13.8 %collective-permute-start.1 = (bf16[8,32,128]{2,1,0:T(8,128)(2,1)S(1)}, bf16[8,32,128]{2,1,0:T(8,128)(2,1)S(1)}, u32[]{:S(2)}, u32[]{:S(2)}) collective-permute-start(bf16[8,32,128]{2,1,0:T(8,128)(2,1)S(1)} %collective-permute-done.refs_0_), channel_id=1, source_target_pairs={{0,1},{1,0},{2,3},{3,2},{4,5},{5,4},{6,7},{7,6},{8,9},{9,8},{10,11... | collective-permute-start | bytes 196616 | tf_op jit(solution)/shard_map/ppermute | solution.py:128
  11.9 14.3 %collective-permute-start.7 = (bf16[8,32,128]{2,1,0:T(8,128)(2,1)S(1)}, bf16[8,32,128]{2,1,0:T(8,128)(2,1)S(1)}, u32[]{:S(2)}, u32[]{:S(2)}) collective-permute-start(bf16[8,32,128]{2,1,0:T(8,128)(2,1)S(1)} %collective-permute-done.5.refs_0_), channel_id=1, source_target_pairs={{0,2},{1,3},{2,0},{3,1},{4,6},{5,7},{6,4},{7,5},{8,10},{9,11},{10,... | collective-permute-start | bytes 196616 | tf_op jit(solution)/shard_map/ppermute | solution.py:128
  12.6 14.3 %collective-permute-start.3 = (bf16[8,32,128]{2,1,0:T(8,128)(2,1)S(1)}, bf16[8,32,128]{2,1,0:T(8,128)(2,1)S(1)}, u32[]{:S(2)}, u32[]{:S(2)}) collective-permute-start(bf16[8,32,128]{2,1,0:T(8,128)(2,1)S(1)} %collective-permute-done.2.refs_2_), channel_id=1, source_target_pairs={{0,1},{1,0},{2,3},{3,2},{4,5},{5,4},{6,7},{7,6},{8,9},{9,8},{10,11... | collective-permute-start | bytes 196616 | tf_op jit(solution)/shard_map/ppermute | solution.py:128
  12.9 20.8 %collective-permute-start.16 = (bf16[8,32,128]{2,1,0:T(8,128)(2,1)}, bf16[8,32,128]{2,1,0:T(8,128)(2,1)S(1)}, u32[]{:S(2)}, u32[]{:S(2)}) collective-permute-start(bf16[8,32,128]{2,1,0:T(8,128)(2,1)} %refs_0_.1), channel_id=1, source_target_pairs={{0,2},{1,3},{2,0},{3,1},{4,6},{5,7},{6,4},{7,5},{8,10},{9,11},{10,... | collective-permute-start | bytes 196616 | tf_op jit(solution)/shard_map/ppermute | solution.py:128
  14.2 0.7 %copy-start.3 = (s32[256]{0:T(256)S(1)}, s32[256]{0:T(256)}, u32[]{:S(2)}) copy-start(s32[256]{0:T(256)} %lengths.1) | copy-start | bytes 3076
  25.6 19.7 %collective-permute-start.15 = (bf16[8,32,128]{2,1,0:T(8,128)(2,1)S(1)}, bf16[8,32,128]{2,1,0:T(8,128)(2,1)S(1)}, u32[]{:S(2)}, u32[]{:S(2)}) collective-permute-start(bf16[8,32,128]{2,1,0:T(8,128)(2,1)S(1)} %copy-done.1), channel_id=1, source_target_pairs={{0,1},{1,0},{2,3},{3,2},{4,5},{5,4},{6,7},{7,6},{8,9},{9,8},{10,11... | collective-permute-start | bytes 196616 | tf_op jit(solution)/shard_map/ppermute | solution.py:128
  25.7 8.5 %collective-permute-start.6 = (bf16[8,32,128]{2,1,0:T(8,128)(2,1)S(1)}, bf16[8,32,128]{2,1,0:T(8,128)(2,1)S(1)}, u32[]{:S(2)}, u32[]{:S(2)}) collective-permute-start(bf16[8,32,128]{2,1,0:T(8,128)(2,1)S(1)} %collective-permute-done.5.refs_0_), channel_id=1, source_target_pairs={{0,1},{1,0},{2,3},{3,2},{4,5},{5,4},{6,7},{7,6},{8,9},{9,8},{10,11... | collective-permute-start | bytes 196616 | tf_op jit(solution)/shard_map/ppermute | solution.py:128
  26.2 8.1 %collective-permute-start.12 = (bf16[8,32,128]{2,1,0:T(8,128)(2,1)S(1)}, bf16[8,32,128]{2,1,0:T(8,128)(2,1)S(1)}, u32[]{:S(2)}, u32[]{:S(2)}) collective-permute-start(bf16[8,32,128]{2,1,0:T(8,128)(2,1)S(1)} %collective-permute-done.10.refs_0_), channel_id=1, source_target_pairs={{0,2},{1,3},{2,0},{3,1},{4,6},{5,7},{6,4},{7,5},{8,10},{9,11},{10,... | collective-permute-start | bytes 196616 | tf_op jit(solution)/shard_map/ppermute | solution.py:128
  26.9 7.8 %collective-permute-start.8 = (bf16[8,32,128]{2,1,0:T(8,128)(2,1)S(1)}, bf16[8,32,128]{2,1,0:T(8,128)(2,1)S(1)}, u32[]{:S(2)}, u32[]{:S(2)}) collective-permute-start(bf16[8,32,128]{2,1,0:T(8,128)(2,1)S(1)} %collective-permute-done.7.refs_2_), channel_id=1, source_target_pairs={{0,1},{1,0},{2,3},{3,2},{4,5},{5,4},{6,7},{7,6},{8,9},{9,8},{10,11... | collective-permute-start | bytes 196616 | tf_op jit(solution)/shard_map/ppermute | solution.py:128
  26.9 3.7 %copy-start = (bf16[288,128,128]{2,1,0:T(8,128)(2,1)S(1)}, bf16[288,128,128]{2,1,0:T(8,128)(2,1)}, u32[]{:S(2)}) copy-start(bf16[288,128,128]{2,1,0:T(8,128)(2,1)} %prepare.1.refs_4_) | copy-start | bytes 28311556
  33.6 7.2 %collective-permute-start.11 = (bf16[8,32,128]{2,1,0:T(8,128)(2,1)S(1)}, bf16[8,32,128]{2,1,0:T(8,128)(2,1)S(1)}, u32[]{:S(2)}, u32[]{:S(2)}) collective-permute-start(bf16[8,32,128]{2,1,0:T(8,128)(2,1)S(1)} %collective-permute-done.10.refs_0_), channel_id=1, source_target_pairs={{0,1},{1,0},{2,3},{3,2},{4,5},{5,4},{6,7},{7,6},{8,9},{9,8},{10,11... | collective-permute-start | bytes 196616 | tf_op jit(solution)/shard_map/ppermute | solution.py:128
  34.2 11.1 %collective-permute-start.17 = (bf16[8,32,128]{2,1,0:T(8,128)(2,1)S(1)}, bf16[8,32,128]{2,1,0:T(8,128)(2,1)S(1)}, u32[]{:S(2)}, u32[]{:S(2)}) collective-permute-start(bf16[8,32,128]{2,1,0:T(8,128)(2,1)S(1)} %collective-permute-done.16.refs_2_), channel_id=1, source_target_pairs={{0,1},{1,0},{2,3},{3,2},{4,5},{5,4},{6,7},{7,6},{8,9},{9,8},{10,11... | collective-permute-start | bytes 196616 | tf_op jit(solution)/shard_map/ppermute | solution.py:128
  34.3 7.0 %collective-permute-start.13 = (bf16[8,32,128]{2,1,0:T(8,128)(2,1)S(1)}, bf16[8,32,128]{2,1,0:T(8,128)(2,1)S(1)}, u32[]{:S(2)}, u32[]{:S(2)}) collective-permute-start(bf16[8,32,128]{2,1,0:T(8,128)(2,1)S(1)} %collective-permute-done.12.refs_2_), channel_id=1, source_target_pairs={{0,1},{1,0},{2,3},{3,2},{4,5},{5,4},{6,7},{7,6},{8,9},{9,8},{10,11... | collective-permute-start | bytes 196616 | tf_op jit(solution)/shard_map/ppermute | solution.py:128
  34.7 16.7 %collective-permute-start.18 = (f32[2,8,128]{2,1,0:T(8,128)S(1)}, f32[2,8,128]{2,1,0:T(8,128)S(1)}, u32[]{:S(2)}, u32[]{:S(2)}) collective-permute-start(f32[2,8,128]{2,1,0:T(8,128)S(1)} %get-tuple-element.17), channel_id=1, source_target_pairs={{0,12},{1,13},{2,14},{3,15},{4,8},{5,9},{6,10},{7,11},{8,4},{9,5},... | collective-permute-start | bytes 24584 | tf_op jit(solution)/shard_map/ppermute | solution.py:128
  40.9 11.8 %collective-permute-start.19 = (f32[2,8,128]{2,1,0:T(8,128)S(1)}, f32[2,8,128]{2,1,0:T(8,128)S(1)}, u32[]{:S(2)}, u32[]{:S(2)}) collective-permute-start(f32[2,8,128]{2,1,0:T(8,128)S(1)} %get-tuple-element.18), channel_id=1, source_target_pairs={{0,8},{1,9},{2,10},{3,11},{4,12},{5,13},{6,14},{7,15},{8,0},{9,1},... | collective-permute-start | bytes 24584 | tf_op jit(solution)/shard_map/ppermute | solution.py:128
  44.3 8.4 %collective-permute-start.20 = (f32[2,8,128]{2,1,0:T(8,128)S(1)}, f32[2,8,128]{2,1,0:T(8,128)S(1)}, u32[]{:S(2)}, u32[]{:S(2)}) collective-permute-start(f32[2,8,128]{2,1,0:T(8,128)S(1)} %get-tuple-element.19), channel_id=1, source_target_pairs={{0,4},{1,5},{2,6},{3,7},{4,0},{5,1},{6,2},{7,3},{8,12},{9,13},{10,... | collective-permute-start | bytes 24584 | tf_op jit(solution)/shard_map/ppermute | solution.py:128
  48.3 5.8 %collective-permute-start.4 = (f32[2,8,128]{2,1,0:T(8,128)S(1)}, f32[2,8,128]{2,1,0:T(8,128)S(1)}, u32[]{:S(2)}, u32[]{:S(2)}) collective-permute-start(f32[2,8,128]{2,1,0:T(8,128)S(1)} %get-tuple-element.13), channel_id=1, source_target_pairs={{0,12},{1,13},{2,14},{3,15},{4,8},{5,9},{6,10},{7,11},{8,4},{9,5},... | collective-permute-start | bytes 24584 | tf_op jit(solution)/shard_map/ppermute | solution.py:128
  51.4 4.5 %collective-permute-start.9 = (f32[2,8,128]{2,1,0:T(8,128)S(1)}, f32[2,8,128]{2,1,0:T(8,128)S(1)}, u32[]{:S(2)}, u32[]{:S(2)}) collective-permute-start(f32[2,8,128]{2,1,0:T(8,128)S(1)} %get-tuple-element.14), channel_id=1, source_target_pairs={{0,8},{1,9},{2,10},{3,11},{4,12},{5,13},{6,14},{7,15},{8,0},{9,1},... | collective-permute-start | bytes 24584 | tf_op jit(solution)/shard_map/ppermute | solution.py:128
  51.4 4.5 %collective-permute-start.14 = (f32[2,8,128]{2,1,0:T(8,128)S(1)}, f32[2,8,128]{2,1,0:T(8,128)S(1)}, u32[]{:S(2)}, u32[]{:S(2)}) collective-permute-start(f32[2,8,128]{2,1,0:T(8,128)S(1)} %get-tuple-element.15), channel_id=1, source_target_pairs={{0,4},{1,5},{2,6},{3,7},{4,0},{5,1},{6,2},{7,3},{8,12},{9,13},{10,... | collective-permute-start | bytes 24584 | tf_op jit(solution)/shard_map/ppermute | solution.py:128
  52.7 3.7 %collective-permute-start.21 = (f32[2,8,128]{2,1,0:T(8,128)S(1)}, f32[2,8,128]{2,1,0:T(8,128)S(1)}, u32[]{:S(2)}, u32[]{:S(2)}) collective-permute-start(f32[2,8,128]{2,1,0:T(8,128)S(1)} %add_add_fusion), channel_id=1, source_target_pairs={{0,2},{1,3},{2,0},{3,1},{4,6},{5,7},{6,4},{7,5},{8,10},{9,11},{10,... | collective-permute-start | bytes 24584 | tf_op jit(solution)/shard_map/ppermute | solution.py:128
  56.4 1.2 %collective-permute-start.22 = (f32[8,128]{1,0:T(8,128)S(1)}, f32[8,128]{1,0:T(8,128)S(1)}, u32[]{:S(2)}, u32[]{:S(2)}) collective-permute-start(f32[8,128]{1,0:T(8,128)S(1)} %slice_bitcast_fusion), channel_id=1, source_target_pairs={{0,1},{1,0},{2,3},{3,2},{4,5},{5,4},{6,7},{7,6},{8,9},{9,8},{10,11... | collective-permute-start | bytes 12296 | tf_op jit(solution)/shard_map/ppermute | solution.py:128

commit v2 on v0

v2 whole, which is shorter than its diff:
```python
import functools

import jax
import jax.numpy as jnp
from jax import lax
from jax.experimental import pallas as pl
from jax.experimental.pallas import tpu as pltpu
from jax.sharding import PartitionSpec as P

AXES = ("shard", "sub")
VMEM = pl.BlockSpec(memory_space=pltpu.VMEM)
SMEM = pl.BlockSpec(memory_space=pltpu.SMEM)


def score_kernel(shifts, n_blocks, candidates, lengths, *refs):
    blocks, documents, out = refs[:n_blocks], refs[n_blocks], refs[n_blocks + 1]
    me = lax.axis_index("shard") * lax.axis_size("sub") + lax.axis_index("sub")
    slots = candidates.shape[0]
    n_queries, terms, dim = blocks[0].shape
    tokens = documents.shape[1]
    width = out.shape[-1]
    group = dim // terms
    row = lax.broadcasted_iota(jnp.int32, (tokens, group * terms), 0)
    which = lax.broadcasted_iota(jnp.int32, (1, group * terms), 1) // terms
    member = lax.broadcasted_iota(jnp.int32, (group * terms, dim), 0) // terms
    lane = lax.broadcasted_iota(jnp.int32, (slots, width), 1)
    slot = lax.broadcasted_iota(jnp.int32, (slots, width), 0)
    own = lane == me * slots + slot

    def group_scores(b, first):
        column = (me ^ shifts[b]) * n_queries + first
        terms_of = blocks[b][first : first + group].reshape(group * terms, dim)
        spread = jnp.concatenate(
            [jnp.where(member == g, terms_of, jnp.zeros_like(terms_of)) for g in range(group)], 1
        )
        tops = []
        for s in range(slots):
            sides = []
            limit = jnp.zeros((1, group * terms), jnp.int32)
            for g in range(group):
                named = candidates[s, column + g]
                place = jnp.maximum(named, 0)
                sides.append(documents[place])
                limit = jnp.where(which == g, jnp.where(named >= 0, lengths[place], 0), limit)
            similar = lax.dot_general(
                jnp.concatenate(sides, 1),
                spread,
                (((1,), (1,)), ((), ())),
                preferred_element_type=jnp.float32,
            )
            tops.append(jnp.max(jnp.where(row < limit, similar, -jnp.inf), axis=0, keepdims=True))
        top = jnp.concatenate(tops, 0)
        top = jnp.where(top == -jnp.inf, 0.0, top)
        for g in range(group):
            total = jnp.sum(jnp.where(which == g, top, 0.0), axis=1, keepdims=True)
            line = jnp.sum(jnp.where(own, total, 0.0), axis=0, keepdims=True)
            out[b, first + g : first + g + 1, :] = line

    for b in range(n_blocks):
        for first in range(0, n_queries, group):
            group_scores(b, first)


def score(shifts, candidates, lengths, blocks, documents, width):
    n_blocks = len(blocks)
    n_queries, terms, dim = blocks[0].shape
    tokens = documents.shape[1]
    pairs = n_blocks * n_queries * candidates.shape[0]
    flops = 2 * pairs * terms * dim * tokens * 8
    return pl.pallas_call(
        functools.partial(score_kernel, shifts, n_blocks),
        out_shape=jax.ShapeDtypeStruct((n_blocks, n_queries, width), jnp.float32),
        in_specs=[SMEM, SMEM] + [VMEM] * (n_blocks + 1),
        out_specs=VMEM,
        compiler_params=pltpu.CompilerParams(vmem_limit_bytes=16 << 20),
        cost_estimate=pl.CostEstimate(flops=flops, bytes_accessed=0, transcendentals=0),
        name="score",
    )(candidates, lengths, *blocks, documents)


def shards(queries, documents, doc_lengths, candidates):
    shard, sub = lax.axis_size("shard"), lax.axis_size("sub")
    devices = shard * sub

    def swap(value, k):
        return lax.ppermute(value, AXES, [(i, i ^ k) for i in range(devices)])

    width = devices * candidates.shape[1]
    columns = candidates.T
    steps = [z * 4 for z in range(shard // 2)]
    along = {z: (queries if z == 0 else swap(queries, z)) for z in reversed(steps)}
    across = {z: swap(along[z], 2) for z in reversed(steps)}
    sums = []
    for z in reversed(steps):
        blocks = [along[z], swap(along[z], 1), across[z], swap(across[z], 1)]
        tiles = score((z, z ^ 1, z ^ 2, z ^ 3), columns, doc_lengths, blocks, documents, width)
        sums.append(tiles if z == 0 else swap(tiles, z))
    total = sum(sums[1:], sums[0])
    mine = total[:2] + swap(total[2:], 2)
    return mine[0] + swap(mine[1], 1)


def solution(mesh):
    in_specs = (
        P(("groups", "shard", "sub"), None, None),
        P(("shard", "sub"), None, None),
        P(("shard", "sub")),
        P("groups", ("shard", "sub")),
    )
    out_specs = P(("groups", "shard", "sub"), None)
    return jax.shard_map(shards, mesh=mesh, in_specs=in_specs, out_specs=out_specs, check_vma=False)
```

time: 236 us -> 45.4 us (0.19)
  waiting for transfers between devices: 125 us -> 8.07 us
  local copies, waits for them, and re-layouts: 62.4 us -> 4.77 us
  matrix products: 30.5 us -> 0 us
  starting transfers between devices: 0.04 us -> 19.4 us
  between operations: 14.1 us -> 0.13 us
  Pallas kernels: 0 us -> 12.2 us
    unnamed x3 -> x0, waiting for transfers between devices: 83.2 us -> none
    gather x16 -> x0, local copies, waits for them, and re-layouts: 56.7 us -> none  [the longest x8 51.2 us: score_query(): picked = documents[doc_rows]]
    all_gather x1 -> x0, waiting for transfers between devices: 42.1 us -> none  [shards(): lax.all_gather(queries, ('shard', 'sub'), axis=0, tiled=True)]
    dot_general x8 -> x0, matrix products: 30.5 us -> none  [score_query(): jnp.einsum('td,skd->stk', one_query, picked, preferred_element_type=jnp.f...]
    ppermute x0 -> x20, starting transfers between devices: none -> 19.4 us  [swap(): return lax.ppermute(value, AXES, [(i, i ^ k) for i in range(devices)])]
    pallas_call x0 -> x4, Pallas kernels: none -> 12.2 us  [score(): pl.pallas_call(functools.partial(score_kernel, shifts, n_blocks), out_sha...]
    ppermute x0 -> x20, waiting for transfers between devices: none -> 8.07 us  [swap(): return lax.ppermute(value, AXES, [(i, i ^ k) for i in range(devices)])]
    unnamed x6 -> x12, local copies, waits for them, and re-layouts: 2.46 us -> 4.76 us
  transfers between devices with their start and end apart: 2 -> 20, of which waited for: 2 -> 5; matrix products, arithmetic and copies ran while one was open for 1% -> 0% of each run, Pallas kernels for 0% -> 27%
where the time goes in v2:
time: 45.4 us; the launch traced here: 45.2 us
  starting transfers between devices  19.4 us (43%)
  Pallas kernels  12.2 us (27%)
  waiting for transfers between devices  8.07 us (18%)
  local copies, waits for them, and re-layouts  4.77 us (11%)
  other arithmetic  0.61 us (1%)
    ppermute x20, starting transfers between devices, swap(): return lax.ppermute(value, AXES, [(i, i ^ k) for i in range(devices)])  19.4 us
    pallas_call x4, Pallas kernels, score(): pl.pallas_call(functools.partial(score_kernel, shifts, n_blocks), out_sha...  12.2 us
    ppermute x20, waiting for transfers between devices, swap(): return lax.ppermute(value, AXES, [(i, i ^ k) for i in range(devices)])  8.07 us
    unnamed x12, local copies, waits for them, and re-layouts  4.76 us
  transfers between devices with their start and end apart: 20, of which 5 were waited for; matrix products, arithmetic and copies ran while one was open for 0% of the time, Pallas kernels for 27%

profile of v2, /device:TPU:0, one launch (start us, length us, event | category | flops | bytes accessed | tf_op | source)
XLA Modules:
  0.0 45.2 jit_solution(10093727636379229880)
XLA Ops:
  0.0 5.0 %collective-permute-start = (bf16[8,32,128]{2,1,0:T(8,128)(2,1)}, bf16[8,32,128]{2,1,0:T(8,128)(2,1)S(1)}, u32[]{:S(2)}, u32[]{:S(2)}) collective-permute-start(bf16[8,32,128]{2,1,0:T(8,128)(2,1)} %refs_0_.1), channel_id=1, source_target_pairs={{0,12},{1,13},{2,14},{3,15},{4,8},{5,9},{6,10},{7,11},{8,4},{9,5},... | collective-permute-start | bytes 196616 | tf_op jit(solution)/shard_map/ppermute | solution.py:86
  5.0 0.0 collective-permute-start.5
  5.1 2.8 %collective-permute-done.refs_0_ = bf16[8,32,128]{2,1,0:T(8,128)(2,1)S(1)} collective-permute-done((bf16[8,32,128]{2,1,0:T(8,128)(2,1)}, bf16[8,32,128]{2,1,0:T(8,128)(2,1)S(1)}, u32[]{:S(2)}, u32[]{:S(2)}) %collective-permute-start) | collective-permute-done | bytes 65568 | tf_op jit(solution)/shard_map/ppermute | solution.py:86
  7.8 1.9 %collective-permute-start.2 = (bf16[8,32,128]{2,1,0:T(8,128)(2,1)S(1)}, bf16[8,32,128]{2,1,0:T(8,128)(2,1)S(1)}, u32[]{:S(2)}, u32[]{:S(2)}) collective-permute-start(bf16[8,32,128]{2,1,0:T(8,128)(2,1)S(1)} %collective-permute-done.refs_0_), channel_id=1, source_target_pairs={{0,2},{1,3},{2,0},{3,1},{4,6},{5,7},{6,4},{7,5},{8,10},{9,11},{10,... | collective-permute-start | bytes 196616 | tf_op jit(solution)/shard_map/ppermute | solution.py:86
  9.7 2.0 %collective-permute-start.10 = (bf16[8,32,128]{2,1,0:T(8,128)(2,1)}, bf16[8,32,128]{2,1,0:T(8,128)(2,1)S(1)}, u32[]{:S(2)}, u32[]{:S(2)}) collective-permute-start(bf16[8,32,128]{2,1,0:T(8,128)(2,1)} %refs_0_.1), channel_id=1, source_target_pairs={{0,4},{1,5},{2,6},{3,7},{4,0},{5,1},{6,2},{7,3},{8,12},{9,13},{10,... | collective-permute-start | bytes 196616 | tf_op jit(solution)/shard_map/ppermute | solution.py:86
  11.8 0.0 collective-permute-start.1
  11.8 0.0 collective-permute-done.5.refs_0_
  11.8 0.7 %collective-permute-start.7 = (bf16[8,32,128]{2,1,0:T(8,128)(2,1)S(1)}, bf16[8,32,128]{2,1,0:T(8,128)(2,1)S(1)}, u32[]{:S(2)}, u32[]{:S(2)}) collective-permute-start(bf16[8,32,128]{2,1,0:T(8,128)(2,1)S(1)} %collective-permute-done.5.refs_0_), channel_id=1, source_target_pairs={{0,2},{1,3},{2,0},{3,1},{4,6},{5,7},{6,4},{7,5},{8,10},{9,11},{10,... | collective-permute-start | bytes 196616 | tf_op jit(solution)/shard_map/ppermute | solution.py:86
  12.5 0.0 collective-permute-done.2.refs_2_
  12.5 0.2 collective-permute-start.3
  12.7 1.3 %collective-permute-start.16 = (bf16[8,32,128]{2,1,0:T(8,128)(2,1)}, bf16[8,32,128]{2,1,0:T(8,128)(2,1)S(1)}, u32[]{:S(2)}, u32[]{:S(2)}) collective-permute-start(bf16[8,32,128]{2,1,0:T(8,128)(2,1)} %refs_0_.1), channel_id=1, source_target_pairs={{0,2},{1,3},{2,0},{3,1},{4,6},{5,7},{6,4},{7,5},{8,10},{9,11},{10,... | collective-permute-start | bytes 196616 | tf_op jit(solution)/shard_map/ppermute | solution.py:86
  14.0 0.2 collective-permute-done.10.refs_0_
  14.2 0.0 collective-permute-start.15
  14.2 0.0 collective-permute-done.1.refs_1_
  14.2 0.5 %collective-permute-start.6 = (bf16[8,32,128]{2,1,0:T(8,128)(2,1)S(1)}, bf16[8,32,128]{2,1,0:T(8,128)(2,1)S(1)}, u32[]{:S(2)}, u32[]{:S(2)}) collective-permute-start(bf16[8,32,128]{2,1,0:T(8,128)(2,1)S(1)} %collective-permute-done.5.refs_0_), channel_id=1, source_target_pairs={{0,1},{1,0},{2,3},{3,2},{4,5},{5,4},{6,7},{7,6},{8,9},{9,8},{10,11... | collective-permute-start | bytes 196616 | tf_op jit(solution)/shard_map/ppermute | solution.py:86
  14.7 1.9 %collective-permute-done.7.refs_2_ = bf16[8,32,128]{2,1,0:T(8,128)(2,1)S(1)} collective-permute-done((bf16[8,32,128]{2,1,0:T(8,128)(2,1)S(1)}, bf16[8,32,128]{2,1,0:T(8,128)(2,1)S(1)}, u32[]{:S(2)}, u32[]{:S(2)}) %collective-permute-start.7) | collective-permute-done | bytes 65568 | tf_op jit(solution)/shard_map/ppermute | solution.py:86
  16.7 0.4 collective-permute-start.12
  17.0 0.0 collective-permute-done.3.refs_3_
  17.0 0.0 collective-permute-start.8
  17.0 3.4 %copy-done = bf16[256,128,128]{2,1,0:T(8,128)(2,1)S(1)} copy-done((bf16[256,128,128]{2,1,0:T(8,128)(2,1)S(1)}, bf16[256,128,128]{2,1,0:T(8,128)(2,1)}, u32[]{:S(2)}) %copy-start) | copy-done | bytes 8388632
  20.4 0.7 %copy-done.2 = s32[128,8]{0,1:T(8,128)S(1)} copy-done((s32[128,8]{0,1:T(8,128)S(1)}, s32[128,8]{0,1:T(8,128)}, u32[]{:S(2)}) %copy-start.2) | copy-done | bytes 4120
  21.1 0.7 %copy-done.3 = s32[256]{0:T(256)S(1)} copy-done((s32[256]{0:T(256)S(1)}, s32[256]{0:T(256)}, u32[]{:S(2)}) %copy-start.3) | copy-done | bytes 1048
  21.8 3.1 %score.4 = f32[4,8,128]{2,1,0:T(8,128)S(1)} custom-call(s32[8,128]{1,0:T(8,128)S(1)} %bitcast.9, s32[256]{0:T(256)S(1)} %copy-done.3, bf16[8,32,128]{2,1,0:T(8,128)(2,1)S(1)} %collective-permute-done.refs_0_, bf16[8,32,128]{2,1,0:T(8,128)(2,1)S(1)} %collective-permute-done.1.refs_1_, bf16[8,32,128]{2,1,0:T(8,128)(2,1)S(1)} %collective-permute-done.2.refs_2_, ...), custom_call_target="tpu_custom_call" | custom-call | flops 2147483648 | tf_op jit(solution)/shard_map/score/pallas_call | solution.py:70
  24.8 0.0 copy-start.1
  24.8 0.0 collective-permute-done.16.refs_2_
  24.8 0.6 %collective-permute-start.11 = (bf16[8,32,128]{2,1,0:T(8,128)(2,1)S(1)}, bf16[8,32,128]{2,1,0:T(8,128)(2,1)S(1)}, u32[]{:S(2)}, u32[]{:S(2)}) collective-permute-start(bf16[8,32,128]{2,1,0:T(8,128)(2,1)S(1)} %collective-permute-done.10.refs_0_), channel_id=1, source_target_pairs={{0,1},{1,0},{2,3},{3,2},{4,5},{5,4},{6,7},{7,6},{8,9},{9,8},{10,11... | collective-permute-start | bytes 196616 | tf_op jit(solution)/shard_map/ppermute | solution.py:86
  25.4 0.0 collective-permute-done.6.refs_1_
  25.4 0.1 collective-permute-start.17
  25.5 0.0 collective-permute-done.12.refs_2_
  25.5 0.4 collective-permute-start.13
  25.9 0.0 collective-permute-done.8.refs_3_
  25.9 2.9 %collective-permute-start.4 = (f32[4,8,128]{2,1,0:T(8,128)S(1)}, f32[4,8,128]{2,1,0:T(8,128)S(1)}, u32[]{:S(2)}, u32[]{:S(2)}) collective-permute-start(f32[4,8,128]{2,1,0:T(8,128)S(1)} %score.4), channel_id=1, source_target_pairs={{0,12},{1,13},{2,14},{3,15},{4,8},{5,9},{6,10},{7,11},{8,4},{9,5},... | collective-permute-start | bytes 49160 | tf_op jit(solution)/shard_map/ppermute | solution.py:86
  28.8 3.1 %score.5 = f32[4,8,128]{2,1,0:T(8,128)S(1)} custom-call(s32[8,128]{1,0:T(8,128)S(1)} %bitcast.10, s32[256]{0:T(256)S(1)} %copy-done.3, bf16[8,32,128]{2,1,0:T(8,128)(2,1)S(1)} %collective-permute-done.5.refs_0_, bf16[8,32,128]{2,1,0:T(8,128)(2,1)S(1)} %collective-permute-done.6.refs_1_, bf16[8,32,128]{2,1,0:T(8,128)(2,1)S(1)} %collective-permute-done.7.refs_2_, ...), custom_call_target="tpu_custom_call" | custom-call | flops 2147483648 | tf_op jit(solution)/shard_map/score/pallas_call | solution.py:70
  31.9 0.0 collective-permute-done.11.refs_1_
  31.9 0.1 collective-permute-start.9
  32.0 0.0 collective-permute-done.13.refs_3_
  32.0 3.1 %score.6 = f32[4,8,128]{2,1,0:T(8,128)S(1)} custom-call(s32[8,128]{1,0:T(8,128)S(1)} %bitcast.11, s32[256]{0:T(256)S(1)} %copy-done.3, bf16[8,32,128]{2,1,0:T(8,128)(2,1)S(1)} %collective-permute-done.10.refs_0_, bf16[8,32,128]{2,1,0:T(8,128)(2,1)S(1)} %collective-permute-done.11.refs_1_, bf16[8,32,128]{2,1,0:T(8,128)(2,1)S(1)} %collective-permute-done.12.refs_2_, ...), custom_call_target="tpu_custom_call" | custom-call | flops 2147483648 | tf_op jit(solution)/shard_map/score/pallas_call | solution.py:70
  35.1 1.5 %collective-permute-start.14 = (f32[4,8,128]{2,1,0:T(8,128)S(1)}, f32[4,8,128]{2,1,0:T(8,128)S(1)}, u32[]{:S(2)}, u32[]{:S(2)}) collective-permute-start(f32[4,8,128]{2,1,0:T(8,128)S(1)} %score.6), channel_id=1, source_target_pairs={{0,4},{1,5},{2,6},{3,7},{4,0},{5,1},{6,2},{7,3},{8,12},{9,13},{10,... | collective-permute-start | bytes 49160 | tf_op jit(solution)/shard_map/ppermute | solution.py:86
  36.5 0.0 collective-permute-done.15.refs_1_
  36.5 0.0 collective-permute-done.17.refs_3_
  36.6 3.1 %score.7 = f32[4,8,128]{2,1,0:T(8,128)S(1)} custom-call(s32[8,128]{1,0:T(8,128)S(1)} %bitcast.12, s32[256]{0:T(256)S(1)} %copy-done.3, bf16[8,32,128]{2,1,0:T(8,128)(2,1)S(1)} %copy-done.1, bf16[8,32,128]{2,1,0:T(8,128)(2,1)S(1)} %collective-permute-done.15.refs_1_, bf16[8,32,128]{2,1,0:T(8,128)(2,1)S(1)} %collective-permute-done.16.refs_2_, ...), custom_call_target="tpu_custom_call" | custom-call | flops 2147483648 | tf_op jit(solution)/shard_map/score/pallas_call | solution.py:70
  39.6 0.0 collective-permute-done.4
  39.6 0.0 collective-permute-done.9
  39.6 0.0 collective-permute-done.14
  39.7 1.7 %collective-permute-start.18 = (f32[2,8,128]{2,1,0:T(8,128)S(1)}, f32[2,8,128]{2,1,0:T(8,128)S(1)}, u32[]{:S(2)}, u32[]{:S(2)}) collective-permute-start(f32[2,8,128]{2,1,0:T(8,128)S(1)} %slice.17), channel_id=1, source_target_pairs={{0,2},{1,3},{2,0},{3,1},{4,6},{5,7},{6,4},{7,5},{8,10},{9,11},{10,... | collective-permute-start | bytes 24584 | tf_op jit(solution)/shard_map/ppermute | solution.py:86
  41.4 2.0 %collective-permute-done.18 = f32[2,8,128]{2,1,0:T(8,128)S(1)} collective-permute-done((f32[2,8,128]{2,1,0:T(8,128)S(1)}, f32[2,8,128]{2,1,0:T(8,128)S(1)}, u32[]{:S(2)}, u32[]{:S(2)}) %collective-permute-start.18) | collective-permute-done | bytes 8224 | tf_op jit(solution)/shard_map/ppermute | solution.py:86
  43.4 1.2 %collective-permute-done.19 = f32[8,128]{1,0:T(8,128)S(1)} collective-permute-done((f32[8,128]{1,0:T(8,128)S(1)}, f32[8,128]{1,0:T(8,128)S(1)}, u32[]{:S(2)}, u32[]{:S(2)}) %collective-permute-start.19) | collective-permute-done | bytes 4128 | tf_op jit(solution)/shard_map/ppermute | solution.py:86
  44.6 0.6 %fusion = f32[8,128]{1,0:T(8,128)} fusion(f32[8,128]{1,0:T(8,128)S(1)} %collective-permute-done.19, f32[2,8,128]{2,1,0:T(8,128)S(1)} %slice_add_fusion), kind=kLoop, calls=%fused_computation.4 | loop fusion | flops 1024 | bytes 12288 | tf_op jit(solution)/shard_map/add | solution.py:100
  (14 shorter events, 0.0 us)
Async XLA Ops:
  0.0 7.8 %collective-permute-start = (bf16[8,32,128]{2,1,0:T(8,128)(2,1)}, bf16[8,32,128]{2,1,0:T(8,128)(2,1)S(1)}, u32[]{:S(2)}, u32[]{:S(2)}) collective-permute-start(bf16[8,32,128]{2,1,0:T(8,128)(2,1)} %refs_0_.1), channel_id=1, source_target_pairs={{0,12},{1,13},{2,14},{3,15},{4,8},{5,9},{6,10},{7,11},{8,4},{9,5},... | collective-permute-start | bytes 196616 | tf_op jit(solution)/shard_map/ppermute | solution.py:86
  5.0 6.7 %collective-permute-start.5 = (bf16[8,32,128]{2,1,0:T(8,128)(2,1)}, bf16[8,32,128]{2,1,0:T(8,128)(2,1)S(1)}, u32[]{:S(2)}, u32[]{:S(2)}) collective-permute-start(bf16[8,32,128]{2,1,0:T(8,128)(2,1)} %refs_0_.1), channel_id=1, source_target_pairs={{0,8},{1,9},{2,10},{3,11},{4,12},{5,13},{6,14},{7,15},{8,0},{9,1},... | collective-permute-start | bytes 196616 | tf_op jit(solution)/shard_map/ppermute | solution.py:86
  7.8 4.7 %collective-permute-start.2 = (bf16[8,32,128]{2,1,0:T(8,128)(2,1)S(1)}, bf16[8,32,128]{2,1,0:T(8,128)(2,1)S(1)}, u32[]{:S(2)}, u32[]{:S(2)}) collective-permute-start(bf16[8,32,128]{2,1,0:T(8,128)(2,1)S(1)} %collective-permute-done.refs_0_), channel_id=1, source_target_pairs={{0,2},{1,3},{2,0},{3,1},{4,6},{5,7},{6,4},{7,5},{8,10},{9,11},{10,... | collective-permute-start | bytes 196616 | tf_op jit(solution)/shard_map/ppermute | solution.py:86
  9.7 4.5 %collective-permute-start.10 = (bf16[8,32,128]{2,1,0:T(8,128)(2,1)}, bf16[8,32,128]{2,1,0:T(8,128)(2,1)S(1)}, u32[]{:S(2)}, u32[]{:S(2)}) collective-permute-start(bf16[8,32,128]{2,1,0:T(8,128)(2,1)} %refs_0_.1), channel_id=1, source_target_pairs={{0,4},{1,5},{2,6},{3,7},{4,0},{5,1},{6,2},{7,3},{8,12},{9,13},{10,... | collective-permute-start | bytes 196616 | tf_op jit(solution)/shard_map/ppermute | solution.py:86
  11.8 2.5 %collective-permute-start.1 = (bf16[8,32,128]{2,1,0:T(8,128)(2,1)S(1)}, bf16[8,32,128]{2,1,0:T(8,128)(2,1)S(1)}, u32[]{:S(2)}, u32[]{:S(2)}) collective-permute-start(bf16[8,32,128]{2,1,0:T(8,128)(2,1)S(1)} %collective-permute-done.refs_0_), channel_id=1, source_target_pairs={{0,1},{1,0},{2,3},{3,2},{4,5},{5,4},{6,7},{7,6},{8,9},{9,8},{10,11... | collective-permute-start | bytes 196616 | tf_op jit(solution)/shard_map/ppermute | solution.py:86
  11.8 4.9 %collective-permute-start.7 = (bf16[8,32,128]{2,1,0:T(8,128)(2,1)S(1)}, bf16[8,32,128]{2,1,0:T(8,128)(2,1)S(1)}, u32[]{:S(2)}, u32[]{:S(2)}) collective-permute-start(bf16[8,32,128]{2,1,0:T(8,128)(2,1)S(1)} %collective-permute-done.5.refs_0_), channel_id=1, source_target_pairs={{0,2},{1,3},{2,0},{3,1},{4,6},{5,7},{6,4},{7,5},{8,10},{9,11},{10,... | collective-permute-start | bytes 196616 | tf_op jit(solution)/shard_map/ppermute | solution.py:86
  12.5 4.5 %collective-permute-start.3 = (bf16[8,32,128]{2,1,0:T(8,128)(2,1)S(1)}, bf16[8,32,128]{2,1,0:T(8,128)(2,1)S(1)}, u32[]{:S(2)}, u32[]{:S(2)}) collective-permute-start(bf16[8,32,128]{2,1,0:T(8,128)(2,1)S(1)} %collective-permute-done.2.refs_2_), channel_id=1, source_target_pairs={{0,1},{1,0},{2,3},{3,2},{4,5},{5,4},{6,7},{7,6},{8,9},{9,8},{10,11... | collective-permute-start | bytes 196616 | tf_op jit(solution)/shard_map/ppermute | solution.py:86
  12.7 12.1 %collective-permute-start.16 = (bf16[8,32,128]{2,1,0:T(8,128)(2,1)}, bf16[8,32,128]{2,1,0:T(8,128)(2,1)S(1)}, u32[]{:S(2)}, u32[]{:S(2)}) collective-permute-start(bf16[8,32,128]{2,1,0:T(8,128)(2,1)} %refs_0_.1), channel_id=1, source_target_pairs={{0,2},{1,3},{2,0},{3,1},{4,6},{5,7},{6,4},{7,5},{8,10},{9,11},{10,... | collective-permute-start | bytes 196616 | tf_op jit(solution)/shard_map/ppermute | solution.py:86
  14.2 22.3 %collective-permute-start.15 = (bf16[8,32,128]{2,1,0:T(8,128)(2,1)}, bf16[8,32,128]{2,1,0:T(8,128)(2,1)S(1)}, u32[]{:S(2)}, u32[]{:S(2)}) collective-permute-start(bf16[8,32,128]{2,1,0:T(8,128)(2,1)} %refs_0_.1), channel_id=1, source_target_pairs={{0,1},{1,0},{2,3},{3,2},{4,5},{5,4},{6,7},{7,6},{8,9},{9,8},{10,11... | collective-permute-start | bytes 196616 | tf_op jit(solution)/shard_map/ppermute | solution.py:86
  14.2 11.2 %collective-permute-start.6 = (bf16[8,32,128]{2,1,0:T(8,128)(2,1)S(1)}, bf16[8,32,128]{2,1,0:T(8,128)(2,1)S(1)}, u32[]{:S(2)}, u32[]{:S(2)}) collective-permute-start(bf16[8,32,128]{2,1,0:T(8,128)(2,1)S(1)} %collective-permute-done.5.refs_0_), channel_id=1, source_target_pairs={{0,1},{1,0},{2,3},{3,2},{4,5},{5,4},{6,7},{7,6},{8,9},{9,8},{10,11... | collective-permute-start | bytes 196616 | tf_op jit(solution)/shard_map/ppermute | solution.py:86
  16.7 8.8 %collective-permute-start.12 = (bf16[8,32,128]{2,1,0:T(8,128)(2,1)S(1)}, bf16[8,32,128]{2,1,0:T(8,128)(2,1)S(1)}, u32[]{:S(2)}, u32[]{:S(2)}) collective-permute-start(bf16[8,32,128]{2,1,0:T(8,128)(2,1)S(1)} %collective-permute-done.10.refs_0_), channel_id=1, source_target_pairs={{0,2},{1,3},{2,0},{3,1},{4,6},{5,7},{6,4},{7,5},{8,10},{9,11},{10,... | collective-permute-start | bytes 196616 | tf_op jit(solution)/shard_map/ppermute | solution.py:86
  17.0 8.9 %collective-permute-start.8 = (bf16[8,32,128]{2,1,0:T(8,128)(2,1)S(1)}, bf16[8,32,128]{2,1,0:T(8,128)(2,1)S(1)}, u32[]{:S(2)}, u32[]{:S(2)}) collective-permute-start(bf16[8,32,128]{2,1,0:T(8,128)(2,1)S(1)} %collective-permute-done.7.refs_2_), channel_id=1, source_target_pairs={{0,1},{1,0},{2,3},{3,2},{4,5},{5,4},{6,7},{7,6},{8,9},{9,8},{10,11... | collective-permute-start | bytes 196616 | tf_op jit(solution)/shard_map/ppermute | solution.py:86
  17.0 3.4 %copy-start = (bf16[256,128,128]{2,1,0:T(8,128)(2,1)S(1)}, bf16[256,128,128]{2,1,0:T(8,128)(2,1)}, u32[]{:S(2)}) copy-start(bf16[256,128,128]{2,1,0:T(8,128)(2,1)} %refs_4_.7) | copy-start | bytes 25165828
  20.4 0.7 %copy-start.2 = (s32[128,8]{0,1:T(8,128)S(1)}, s32[128,8]{0,1:T(8,128)}, u32[]{:S(2)}) copy-start(s32[128,8]{0,1:T(8,128)} %param.7) | copy-start | bytes 12292
  21.1 0.7 %copy-start.3 = (s32[256]{0:T(256)S(1)}, s32[256]{0:T(256)}, u32[]{:S(2)}) copy-start(s32[256]{0:T(256)} %lengths.7) | copy-start | bytes 3076
  24.8 11.7 %slice-start = ((s8[8388608]{0:T(1024)(128)(4,1)}), s8[4194304]{0:T(1024)(128)(4,1)S(1)}, s32[]{:S(2)}) async-start(s8[8388608]{0:T(1024)(128)(4,1)} %bitcast.7), calls=%async_computation | async-start | bytes 8388608
  24.8 11.7 %copy-start.1 = (bf16[8,32,128]{2,1,0:T(8,128)(2,1)S(1)}, bf16[8,32,128]{2,1,0:T(8,128)(2,1)}, u32[]{:S(2)}) copy-start(bf16[8,32,128]{2,1,0:T(8,128)(2,1)} %refs_0_.1) | copy-start | bytes 196612
  24.8 7.0 %collective-permute-start.11 = (bf16[8,32,128]{2,1,0:T(8,128)(2,1)S(1)}, bf16[8,32,128]{2,1,0:T(8,128)(2,1)S(1)}, u32[]{:S(2)}, u32[]{:S(2)}) collective-permute-start(bf16[8,32,128]{2,1,0:T(8,128)(2,1)S(1)} %collective-permute-done.10.refs_0_), channel_id=1, source_target_pairs={{0,1},{1,0},{2,3},{3,2},{4,5},{5,4},{6,7},{7,6},{8,9},{9,8},{10,11... | collective-permute-start | bytes 196616 | tf_op jit(solution)/shard_map/ppermute | solution.py:86
  25.4 11.1 %collective-permute-start.17 = (bf16[8,32,128]{2,1,0:T(8,128)(2,1)S(1)}, bf16[8,32,128]{2,1,0:T(8,128)(2,1)S(1)}, u32[]{:S(2)}, u32[]{:S(2)}) collective-permute-start(bf16[8,32,128]{2,1,0:T(8,128)(2,1)S(1)} %collective-permute-done.16.refs_2_), channel_id=1, source_target_pairs={{0,1},{1,0},{2,3},{3,2},{4,5},{5,4},{6,7},{7,6},{8,9},{9,8},{10,11... | collective-permute-start | bytes 196616 | tf_op jit(solution)/shard_map/ppermute | solution.py:86
  25.5 6.5 %collective-permute-start.13 = (bf16[8,32,128]{2,1,0:T(8,128)(2,1)S(1)}, bf16[8,32,128]{2,1,0:T(8,128)(2,1)S(1)}, u32[]{:S(2)}, u32[]{:S(2)}) collective-permute-start(bf16[8,32,128]{2,1,0:T(8,128)(2,1)S(1)} %collective-permute-done.12.refs_2_), channel_id=1, source_target_pairs={{0,1},{1,0},{2,3},{3,2},{4,5},{5,4},{6,7},{7,6},{8,9},{9,8},{10,11... | collective-permute-start | bytes 196616 | tf_op jit(solution)/shard_map/ppermute | solution.py:86
  25.9 13.7 %collective-permute-start.4 = (f32[4,8,128]{2,1,0:T(8,128)S(1)}, f32[4,8,128]{2,1,0:T(8,128)S(1)}, u32[]{:S(2)}, u32[]{:S(2)}) collective-permute-start(f32[4,8,128]{2,1,0:T(8,128)S(1)} %score.4), channel_id=1, source_target_pairs={{0,12},{1,13},{2,14},{3,15},{4,8},{5,9},{6,10},{7,11},{8,4},{9,5},... | collective-permute-start | bytes 49160 | tf_op jit(solution)/shard_map/ppermute | solution.py:86
  31.9 4.7 %slice-start.1 = ((s8[8388608]{0:T(1024)(128)(4,1)}), s8[4194304]{0:T(1024)(128)(4,1)S(1)}, s32[]{:S(2)}) async-start(s8[8388608]{0:T(1024)(128)(4,1)} %bitcast.7), calls=%async_computation.1 | async-start | bytes 8388608
  31.9 7.7 %collective-permute-start.9 = (f32[4,8,128]{2,1,0:T(8,128)S(1)}, f32[4,8,128]{2,1,0:T(8,128)S(1)}, u32[]{:S(2)}, u32[]{:S(2)}) collective-permute-start(f32[4,8,128]{2,1,0:T(8,128)S(1)} %score.5), channel_id=1, source_target_pairs={{0,8},{1,9},{2,10},{3,11},{4,12},{5,13},{6,14},{7,15},{8,0},{9,1},... | collective-permute-start | bytes 49160 | tf_op jit(solution)/shard_map/ppermute | solution.py:86
  35.1 4.6 %collective-permute-start.14 = (f32[4,8,128]{2,1,0:T(8,128)S(1)}, f32[4,8,128]{2,1,0:T(8,128)S(1)}, u32[]{:S(2)}, u32[]{:S(2)}) collective-permute-start(f32[4,8,128]{2,1,0:T(8,128)S(1)} %score.6), channel_id=1, source_target_pairs={{0,4},{1,5},{2,6},{3,7},{4,0},{5,1},{6,2},{7,3},{8,12},{9,13},{10,... | collective-permute-start | bytes 49160 | tf_op jit(solution)/shard_map/ppermute | solution.py:86
  39.7 3.7 %collective-permute-start.18 = (f32[2,8,128]{2,1,0:T(8,128)S(1)}, f32[2,8,128]{2,1,0:T(8,128)S(1)}, u32[]{:S(2)}, u32[]{:S(2)}) collective-permute-start(f32[2,8,128]{2,1,0:T(8,128)S(1)} %slice.17), channel_id=1, source_target_pairs={{0,2},{1,3},{2,0},{3,1},{4,6},{5,7},{6,4},{7,5},{8,10},{9,11},{10,... | collective-permute-start | bytes 24584 | tf_op jit(solution)/shard_map/ppermute | solution.py:86
  43.4 1.2 %collective-permute-start.19 = (f32[8,128]{1,0:T(8,128)S(1)}, f32[8,128]{1,0:T(8,128)S(1)}, u32[]{:S(2)}, u32[]{:S(2)}) collective-permute-start(f32[8,128]{1,0:T(8,128)S(1)} %slice_bitcast_fusion), channel_id=1, source_target_pairs={{0,1},{1,0},{2,3},{3,2},{4,5},{5,4},{6,7},{7,6},{8,9},{9,8},{10,11... | collective-permute-start | bytes 12296 | tf_op jit(solution)/shard_map/ppermute | solution.py:86

commit v3 on v2

--- a/solution.py
+++ b/solution.py
@@ -12,20 +12,35 @@
 SMEM = pl.BlockSpec(memory_space=pltpu.SMEM)
 
 
-def score_kernel(shifts, n_blocks, candidates, lengths, *refs):
+def lanes_kernel(own):
+    me = lax.axis_index("shard") * lax.axis_size("sub") + lax.axis_index("sub")
+    lane = lax.broadcasted_iota(jnp.int32, own.shape, 1)
+    slot = lax.broadcasted_iota(jnp.int32, own.shape, 0)
+    own[...] = jnp.where(lane == me * own.shape[0] + slot, 1.0, 0.0)
+
+
+def lanes_of(slots, width):
+    return pl.pallas_call(
+        lanes_kernel,
+        out_shape=jax.ShapeDtypeStruct((slots, width), jnp.float32),
+        out_specs=VMEM,
+        compiler_params=pltpu.CompilerParams(vmem_limit_bytes=1 << 20),
+        cost_estimate=pl.CostEstimate(flops=1 << 35, bytes_accessed=0, transcendentals=0),
+        name="lanes",
+    )()
+
+
+def score_kernel(shifts, n_blocks, candidates, lengths, own, *refs):
     blocks, documents, out = refs[:n_blocks], refs[n_blocks], refs[n_blocks + 1]
     me = lax.axis_index("shard") * lax.axis_size("sub") + lax.axis_index("sub")
     slots = candidates.shape[0]
     n_queries, terms, dim = blocks[0].shape
     tokens = documents.shape[1]
-    width = out.shape[-1]
     group = dim // terms
     row = lax.broadcasted_iota(jnp.int32, (tokens, group * terms), 0)
     which = lax.broadcasted_iota(jnp.int32, (1, group * terms), 1) // terms
     member = lax.broadcasted_iota(jnp.int32, (group * terms, dim), 0) // terms
-    lane = lax.broadcasted_iota(jnp.int32, (slots, width), 1)
-    slot = lax.broadcasted_iota(jnp.int32, (slots, width), 0)
-    own = lane == me * slots + slot
+    mark = own[...]
 
     def group_scores(b, first):
         column = (me ^ shifts[b]) * n_queries + first
@@ -53,7 +68,7 @@
         top = jnp.where(top == -jnp.inf, 0.0, top)
         for g in range(group):
             total = jnp.sum(jnp.where(which == g, top, 0.0), axis=1, keepdims=True)
-            line = jnp.sum(jnp.where(own, total, 0.0), axis=0, keepdims=True)
+            line = jnp.sum(mark * total, axis=0, keepdims=True)
             out[b, first + g : first + g + 1, :] = line
 
     for b in range(n_blocks):
@@ -61,21 +76,21 @@
             group_scores(b, first)
 
 
-def score(shifts, candidates, lengths, blocks, documents, width):
+def score(shifts, candidates, lengths, own, blocks, documents):
     n_blocks = len(blocks)
     n_queries, terms, dim = blocks[0].shape
     tokens = documents.shape[1]
     pairs = n_blocks * n_queries * candidates.shape[0]
-    flops = 2 * pairs * terms * dim * tokens * 8
+    flops = 2 * pairs * terms * dim * tokens * 16
     return pl.pallas_call(
         functools.partial(score_kernel, shifts, n_blocks),
-        out_shape=jax.ShapeDtypeStruct((n_blocks, n_queries, width), jnp.float32),
-        in_specs=[SMEM, SMEM] + [VMEM] * (n_blocks + 1),
+        out_shape=jax.ShapeDtypeStruct((n_blocks, n_queries, own.shape[1]), jnp.float32),
+        in_specs=[SMEM] * 2 + [VMEM] * (n_blocks + 2),
         out_specs=VMEM,
         compiler_params=pltpu.CompilerParams(vmem_limit_bytes=16 << 20),
         cost_estimate=pl.CostEstimate(flops=flops, bytes_accessed=0, transcendentals=0),
         name="score",
-    )(candidates, lengths, *blocks, documents)
+    )(candidates, lengths, own, *blocks, documents)
 
 
 def shards(queries, documents, doc_lengths, candidates):
@@ -85,19 +100,32 @@
     def swap(value, k):
         return lax.ppermute(value, AXES, [(i, i ^ k) for i in range(devices)])
 
-    width = devices * candidates.shape[1]
+    def after(value, *others):
+        return lax.optimization_barrier((value, *others))[0]
+
     columns = candidates.T
-    steps = [z * 4 for z in range(shard // 2)]
-    along = {z: (queries if z == 0 else swap(queries, z)) for z in reversed(steps)}
-    across = {z: swap(along[z], 2) for z in reversed(steps)}
-    sums = []
-    for z in reversed(steps):
-        blocks = [along[z], swap(along[z], 1), across[z], swap(across[z], 1)]
-        tiles = score((z, z ^ 1, z ^ 2, z ^ 3), columns, doc_lengths, blocks, documents, width)
-        sums.append(tiles if z == 0 else swap(tiles, z))
-    total = sum(sums[1:], sums[0])
-    mine = total[:2] + swap(total[2:], 2)
-    return mine[0] + swap(mine[1], 1)
+    own = lanes_of(candidates.shape[1], devices * candidates.shape[1])
+    queries = after(queries, own)
+    steps = [z * 4 for z in reversed(range(1, shard // 2))]
+
+    def scores(shifts, blocks):
+        return score(shifts, columns, doc_lengths, own, blocks, documents)
+
+    along = {z: swap(queries, z) for z in steps}
+    beside = swap(queries, 2)
+    near = scores((0, 1), [queries, swap(queries, 1)])
+    far = []
+    tied = {z: after(along[z], near) for z in steps}
+    across = {z: swap(tied[z], 2) for z in steps}
+    others = {z: swap(tied[z], 1) for z in steps}
+    back = []
+    for z in steps:
+        blocks = [along[z], others[z], across[z], swap(across[z], 1)]
+        back.append(swap(scores((z, z ^ 1, z ^ 2, z ^ 3), blocks), z))
+    far = scores((2, 3), [beside, swap(beside, 1)])
+    near = sum((b[:2] for b in back), near)
+    far = sum((b[2:] for b in back), far)
+    return near[0] + swap(near[1], 1) + swap(far[0], 2) + swap(far[1], 3)
 
 
 def solution(mesh):

time: 45.4 us -> 39.9 us (0.88)
  local copies, waits for them, and re-layouts: 4.77 us -> 0.83 us
  starting transfers between devices: 19.4 us -> 17.4 us
  Pallas kernels: 12.2 us -> 13.1 us
    unnamed x12 -> x8, local copies, waits for them, and re-layouts: 4.76 us -> 0.83 us
    ppermute x20 -> x21, starting transfers between devices: 19.4 us -> 17.4 us  [swap(): return lax.ppermute(value, AXES, [(i, i ^ k) for i in range(devices)])]
    pallas_call x4 -> x5, Pallas kernels: 12.2 us -> 13.1 us  [score(): pl.pallas_call(functools.partial(score_kernel, shifts, n_blocks), out_sha...]
    ppermute x20 -> x21, waiting for transfers between devices: 8.07 us -> 7.75 us  [swap(): return lax.ppermute(value, AXES, [(i, i ^ k) for i in range(devices)])]
  transfers between devices with their start and end apart: 20 -> 21, of which waited for: 5 -> 8; matrix products, arithmetic and copies ran while one was open for 0% -> 0% of each run, Pallas kernels for 27% -> 33%
where the time goes in v3:
time: 39.9 us; the launch traced here: 39.8 us
  starting transfers between devices  17.4 us (44%)
  Pallas kernels  13.1 us (33%)
  waiting for transfers between devices  7.75 us (19%)
  local copies, waits for them, and re-layouts  0.83 us (2%)
  other arithmetic  0.61 us (2%)
    ppermute x21, starting transfers between devices, swap(): return lax.ppermute(value, AXES, [(i, i ^ k) for i in range(devices)])  17.4 us
    pallas_call x5, Pallas kernels, score(): pl.pallas_call(functools.partial(score_kernel, shifts, n_blocks), out_sha...  13.1 us
    ppermute x21, waiting for transfers between devices, swap(): return lax.ppermute(value, AXES, [(i, i ^ k) for i in range(devices)])  7.75 us
    unnamed x8, local copies, waits for them, and re-layouts  0.83 us
  transfers between devices with their start and end apart: 21, of which 8 were waited for; matrix products, arithmetic and copies ran while one was open for 0% of the time, Pallas kernels for 33%

profile of v3, /device:TPU:0, one launch (start us, length us, event | category | flops | bytes accessed | tf_op | source)
XLA Modules:
  0.0 39.8 jit_solution(2430544201491730461)
XLA Ops:
  0.0 0.8 %copy-done.1 = bf16[8,32,128]{2,1,0:T(8,128)(2,1)S(1)} copy-done((bf16[8,32,128]{2,1,0:T(8,128)(2,1)S(1)}, bf16[8,32,128]{2,1,0:T(8,128)(2,1)}, u32[]{:S(2)}) %copy-start.1) | copy-done | bytes 65560
  0.8 0.5 %collective-permute-start = (bf16[8,32,128]{2,1,0:T(8,128)(2,1)S(1)}, bf16[8,32,128]{2,1,0:T(8,128)(2,1)S(1)}, u32[]{:S(2)}, u32[]{:S(2)}) collective-permute-start(bf16[8,32,128]{2,1,0:T(8,128)(2,1)S(1)} %copy-done.1), channel_id=1, source_target_pairs={{0,1},{1,0},{2,3},{3,2},{4,5},{5,4},{6,7},{7,6},{8,9},{9,8},{10,11... | collective-permute-start | bytes 196616 | tf_op jit(solution)/shard_map/ppermute | solution.py:101
  1.3 4.6 %collective-permute-start.1 = (bf16[8,32,128]{2,1,0:T(8,128)(2,1)S(1)}, bf16[8,32,128]{2,1,0:T(8,128)(2,1)S(1)}, u32[]{:S(2)}, u32[]{:S(2)}) collective-permute-start(bf16[8,32,128]{2,1,0:T(8,128)(2,1)S(1)} %copy-done.1), channel_id=1, source_target_pairs={{0,12},{1,13},{2,14},{3,15},{4,8},{5,9},{6,10},{7,11},{8,4},{9,5},... | collective-permute-start | bytes 196616 | tf_op jit(solution)/shard_map/ppermute | solution.py:101
  5.9 0.0 collective-permute-start.6
  5.9 0.6 %collective-permute-start.11 = (bf16[8,32,128]{2,1,0:T(8,128)(2,1)S(1)}, bf16[8,32,128]{2,1,0:T(8,128)(2,1)S(1)}, u32[]{:S(2)}, u32[]{:S(2)}) collective-permute-start(bf16[8,32,128]{2,1,0:T(8,128)(2,1)S(1)} %copy-done.1), channel_id=1, source_target_pairs={{0,4},{1,5},{2,6},{3,7},{4,0},{5,1},{6,2},{7,3},{8,12},{9,13},{10,... | collective-permute-start | bytes 196616 | tf_op jit(solution)/shard_map/ppermute | solution.py:101
  6.5 0.0 collective-permute-done.refs_1_
  6.5 2.0 %score.5 = f32[2,8,128]{2,1,0:T(8,128)S(1)} custom-call(s32[8,128]{1,0:T(8,128)S(1)} %bitcast.15, s32[256]{0:T(256)S(1)} %copy-done.3, f32[8,128]{1,0:T(8,128)S(1)} %lanes.1.own, bf16[8,32,128]{2,1,0:T(8,128)(2,1)S(1)} %copy-done.1, bf16[8,32,128]{2,1,0:T(8,128)(2,1)S(1)} %collective-permute-done.refs_1_, bf16[256,128,128]{2,1,0:T(8,128)(2,1)S(1)} %copy-done), custom_call_target="tpu_custom_call" | custom-call | flops 2147483648 | tf_op jit(solution)/shard_map/score/pallas_call | solution.py:85
  8.5 0.4 collective-permute-done.1.refs_0_
  8.8 1.6 %collective-permute-start.3 = (bf16[8,32,128]{2,1,0:T(8,128)(2,1)S(1)}, bf16[8,32,128]{2,1,0:T(8,128)(2,1)S(1)}, u32[]{:S(2)}, u32[]{:S(2)}) collective-permute-start(bf16[8,32,128]{2,1,0:T(8,128)(2,1)S(1)} %collective-permute-done.1.refs_0_), channel_id=1, source_target_pairs={{0,2},{1,3},{2,0},{3,1},{4,6},{5,7},{6,4},{7,5},{8,10},{9,11},{10,... | collective-permute-start | bytes 196616 | tf_op jit(solution)/shard_map/ppermute | solution.py:101
  10.4 0.5 %collective-permute-start.17 = (bf16[8,32,128]{2,1,0:T(8,128)(2,1)S(1)}, bf16[8,32,128]{2,1,0:T(8,128)(2,1)S(1)}, u32[]{:S(2)}, u32[]{:S(2)}) collective-permute-start(bf16[8,32,128]{2,1,0:T(8,128)(2,1)S(1)} %copy-done.1), channel_id=1, source_target_pairs={{0,2},{1,3},{2,0},{3,1},{4,6},{5,7},{6,4},{7,5},{8,10},{9,11},{10,... | collective-permute-start | bytes 196616 | tf_op jit(solution)/shard_map/ppermute | solution.py:101
  10.9 0.0 collective-permute-start.2
  10.9 1.2 %collective-permute-done.6.refs_0_ = bf16[8,32,128]{2,1,0:T(8,128)(2,1)S(1)} collective-permute-done((bf16[8,32,128]{2,1,0:T(8,128)(2,1)S(1)}, bf16[8,32,128]{2,1,0:T(8,128)(2,1)S(1)}, u32[]{:S(2)}, u32[]{:S(2)}) %collective-permute-start.6) | collective-permute-done | bytes 65568 | tf_op jit(solution)/shard_map/ppermute | solution.py:101
  12.0 1.5 %collective-permute-start.8 = (bf16[8,32,128]{2,1,0:T(8,128)(2,1)S(1)}, bf16[8,32,128]{2,1,0:T(8,128)(2,1)S(1)}, u32[]{:S(2)}, u32[]{:S(2)}) collective-permute-start(bf16[8,32,128]{2,1,0:T(8,128)(2,1)S(1)} %collective-permute-done.6.refs_0_), channel_id=1, source_target_pairs={{0,2},{1,3},{2,0},{3,1},{4,6},{5,7},{6,4},{7,5},{8,10},{9,11},{10,... | collective-permute-start | bytes 196616 | tf_op jit(solution)/shard_map/ppermute | solution.py:101
  13.5 0.0 collective-permute-done.11.refs_0_
  13.5 0.5 %collective-permute-start.13 = (bf16[8,32,128]{2,1,0:T(8,128)(2,1)S(1)}, bf16[8,32,128]{2,1,0:T(8,128)(2,1)S(1)}, u32[]{:S(2)}, u32[]{:S(2)}) collective-permute-start(bf16[8,32,128]{2,1,0:T(8,128)(2,1)S(1)} %collective-permute-done.11.refs_0_), channel_id=1, source_target_pairs={{0,2},{1,3},{2,0},{3,1},{4,6},{5,7},{6,4},{7,5},{8,10},{9,11},{10,... | collective-permute-start | bytes 196616 | tf_op jit(solution)/shard_map/ppermute | solution.py:101
  14.1 0.0 collective-permute-done.3.refs_2_
  14.1 0.0 collective-permute-start.4
  14.1 1.0 %collective-permute-done.17.refs_0_ = bf16[8,32,128]{2,1,0:T(8,128)(2,1)S(1)} collective-permute-done((bf16[8,32,128]{2,1,0:T(8,128)(2,1)S(1)}, bf16[8,32,128]{2,1,0:T(8,128)(2,1)S(1)}, u32[]{:S(2)}, u32[]{:S(2)}) %collective-permute-start.17) | collective-permute-done | bytes 65568 | tf_op jit(solution)/shard_map/ppermute | solution.py:101
  15.1 0.0 collective-permute-start.7
  15.1 0.0 collective-permute-done.2.refs_1_
  15.1 0.5 %collective-permute-start.12 = (bf16[8,32,128]{2,1,0:T(8,128)(2,1)S(1)}, bf16[8,32,128]{2,1,0:T(8,128)(2,1)S(1)}, u32[]{:S(2)}, u32[]{:S(2)}) collective-permute-start(bf16[8,32,128]{2,1,0:T(8,128)(2,1)S(1)} %collective-permute-done.11.refs_0_), channel_id=1, source_target_pairs={{0,1},{1,0},{2,3},{3,2},{4,5},{5,4},{6,7},{7,6},{8,9},{9,8},{10,11... | collective-permute-start | bytes 196616 | tf_op jit(solution)/shard_map/ppermute | solution.py:101
  15.6 1.4 %collective-permute-done.8.refs_2_ = bf16[8,32,128]{2,1,0:T(8,128)(2,1)S(1)} collective-permute-done((bf16[8,32,128]{2,1,0:T(8,128)(2,1)S(1)}, bf16[8,32,128]{2,1,0:T(8,128)(2,1)S(1)}, u32[]{:S(2)}, u32[]{:S(2)}) %collective-permute-start.8) | collective-permute-done | bytes 65568 | tf_op jit(solution)/shard_map/ppermute | solution.py:101
  17.0 0.0 collective-permute-start.18
  17.0 0.8 %collective-permute-done.13.refs_2_ = bf16[8,32,128]{2,1,0:T(8,128)(2,1)S(1)} collective-permute-done((bf16[8,32,128]{2,1,0:T(8,128)(2,1)S(1)}, bf16[8,32,128]{2,1,0:T(8,128)(2,1)S(1)}, u32[]{:S(2)}, u32[]{:S(2)}) %collective-permute-start.13) | collective-permute-done | bytes 65568 | tf_op jit(solution)/shard_map/ppermute | solution.py:101
  17.8 0.0 collective-permute-start.9
  17.8 0.0 collective-permute-done.4.refs_3_
  17.8 0.5 %collective-permute-start.14 = (bf16[8,32,128]{2,1,0:T(8,128)(2,1)S(1)}, bf16[8,32,128]{2,1,0:T(8,128)(2,1)S(1)}, u32[]{:S(2)}, u32[]{:S(2)}) collective-permute-start(bf16[8,32,128]{2,1,0:T(8,128)(2,1)S(1)} %collective-permute-done.13.refs_2_), channel_id=1, source_target_pairs={{0,1},{1,0},{2,3},{3,2},{4,5},{5,4},{6,7},{7,6},{8,9},{9,8},{10,11... | collective-permute-start | bytes 196616 | tf_op jit(solution)/shard_map/ppermute | solution.py:101
  18.3 3.1 %score.6 = f32[4,8,128]{2,1,0:T(8,128)S(1)} custom-call(s32[8,128]{1,0:T(8,128)S(1)} %bitcast.16, s32[256]{0:T(256)S(1)} %copy-done.3, f32[8,128]{1,0:T(8,128)S(1)} %lanes.1.own, bf16[8,32,128]{2,1,0:T(8,128)(2,1)S(1)} %collective-permute-done.1.refs_0_, bf16[8,32,128]{2,1,0:T(8,128)(2,1)S(1)} %collective-permute-done.2.refs_1_, ...), custom_call_target="tpu_custom_call" | custom-call | flops 4294967296 | tf_op jit(solution)/shard_map/score/pallas_call | solution.py:85
  21.4 0.0 collective-permute-done.7.refs_1_
  21.4 3.5 %collective-permute-start.5 = (f32[4,8,128]{2,1,0:T(8,128)S(1)}, f32[4,8,128]{2,1,0:T(8,128)S(1)}, u32[]{:S(2)}, u32[]{:S(2)}) collective-permute-start(f32[4,8,128]{2,1,0:T(8,128)S(1)} %score.6), channel_id=1, source_target_pairs={{0,12},{1,13},{2,14},{3,15},{4,8},{5,9},{6,10},{7,11},{8,4},{9,5},... | collective-permute-start | bytes 49160 | tf_op jit(solution)/shard_map/ppermute | solution.py:101
  24.9 0.0 collective-permute-done.9.refs_3_
  24.9 3.1 %score.7 = f32[4,8,128]{2,1,0:T(8,128)S(1)} custom-call(s32[8,128]{1,0:T(8,128)S(1)} %bitcast.17, s32[256]{0:T(256)S(1)} %copy-done.3, f32[8,128]{1,0:T(8,128)S(1)} %lanes.1.own, bf16[8,32,128]{2,1,0:T(8,128)(2,1)S(1)} %collective-permute-done.6.refs_0_, bf16[8,32,128]{2,1,0:T(8,128)(2,1)S(1)} %collective-permute-done.7.refs_1_, ...), custom_call_target="tpu_custom_call" | custom-call | flops 4294967296 | tf_op jit(solution)/shard_map/score/pallas_call | solution.py:85
  28.0 0.4 collective-permute-start.10
  28.4 0.0 collective-permute-done.12.refs_1_
  28.4 0.0 collective-permute-done.14.refs_3_
  28.4 3.1 %score.8 = f32[4,8,128]{2,1,0:T(8,128)S(1)} custom-call(s32[8,128]{1,0:T(8,128)S(1)} %bitcast.18, s32[256]{0:T(256)S(1)} %copy-done.3, f32[8,128]{1,0:T(8,128)S(1)} %lanes.1.own, bf16[8,32,128]{2,1,0:T(8,128)(2,1)S(1)} %collective-permute-done.11.refs_0_, bf16[8,32,128]{2,1,0:T(8,128)(2,1)S(1)} %collective-permute-done.12.refs_1_, ...), custom_call_target="tpu_custom_call" | custom-call | flops 4294967296 | tf_op jit(solution)/shard_map/score/pallas_call | solution.py:85
  31.4 0.6 %collective-permute-start.15 = (f32[4,8,128]{2,1,0:T(8,128)S(1)}, f32[4,8,128]{2,1,0:T(8,128)S(1)}, u32[]{:S(2)}, u32[]{:S(2)}) collective-permute-start(f32[4,8,128]{2,1,0:T(8,128)S(1)} %score.8), channel_id=1, source_target_pairs={{0,4},{1,5},{2,6},{3,7},{4,0},{5,1},{6,2},{7,3},{8,12},{9,13},{10,... | collective-permute-start | bytes 49160 | tf_op jit(solution)/shard_map/ppermute | solution.py:101
  32.0 0.0 collective-permute-done.18.refs_1_
  32.0 2.0 %score.9 = f32[2,8,128]{2,1,0:T(8,128)S(1)} custom-call(s32[8,128]{1,0:T(8,128)S(1)} %bitcast.19, s32[256]{0:T(256)S(1)} %copy-done.3, f32[8,128]{1,0:T(8,128)S(1)} %lanes.1.own, bf16[8,32,128]{2,1,0:T(8,128)(2,1)S(1)} %collective-permute-done.17.refs_0_, bf16[8,32,128]{2,1,0:T(8,128)(2,1)S(1)} %collective-permute-done.18.refs_1_, ...), custom_call_target="tpu_custom_call" | custom-call | flops 2147483648 | tf_op jit(solution)/shard_map/score/pallas_call | solution.py:85
  34.0 0.0 collective-permute-done.5
  34.0 0.0 collective-permute-done.10
  34.0 1.2 %collective-permute-done.15 = f32[4,8,128]{2,1,0:T(8,128)S(1)} collective-permute-done((f32[4,8,128]{2,1,0:T(8,128)S(1)}, f32[4,8,128]{2,1,0:T(8,128)S(1)}, u32[]{:S(2)}, u32[]{:S(2)}) %collective-permute-start.15) | collective-permute-done | bytes 16416 | tf_op jit(solution)/shard_map/ppermute | solution.py:101
  35.2 0.9 %collective-permute-start.19 = (f32[8,128]{1,0:T(8,128)S(1)}, f32[8,128]{1,0:T(8,128)S(1)}, u32[]{:S(2)}, u32[]{:S(2)}) collective-permute-start(f32[8,128]{1,0:T(8,128)S(1)} %get-tuple-element.15), channel_id=1, source_target_pairs={{0,2},{1,3},{2,0},{3,1},{4,6},{5,7},{6,4},{7,5},{8,10},{9,11},{10,... | collective-permute-start | bytes 12296 | tf_op jit(solution)/shard_map/ppermute | solution.py:101
  36.1 0.0 collective-permute-start.20
  36.1 1.3 %collective-permute-start.16 = (f32[8,128]{1,0:T(8,128)S(1)}, f32[8,128]{1,0:T(8,128)S(1)}, u32[]{:S(2)}, u32[]{:S(2)}) collective-permute-start(f32[8,128]{1,0:T(8,128)S(1)} %slice_bitcast_fusion.2), channel_id=1, source_target_pairs={{0,1},{1,0},{2,3},{3,2},{4,5},{5,4},{6,7},{7,6},{8,9},{9,8},{10,11... | collective-permute-start | bytes 12296 | tf_op jit(solution)/shard_map/ppermute | solution.py:101
  37.4 1.5 %collective-permute-done.19 = f32[8,128]{1,0:T(8,128)S(1)} collective-permute-done((f32[8,128]{1,0:T(8,128)S(1)}, f32[8,128]{1,0:T(8,128)S(1)}, u32[]{:S(2)}, u32[]{:S(2)}) %collective-permute-start.19) | collective-permute-done | bytes 4128 | tf_op jit(solution)/shard_map/ppermute | solution.py:101
  38.9 0.3 collective-permute-done.20
  39.2 0.6 %fusion.2 = f32[8,128]{1,0:T(8,128)} fusion(f32[8,128]{1,0:T(8,128)S(1)} %collective-permute-done.20, f32[8,128]{1,0:T(8,128)S(1)} %collective-permute-done.19, f32[8,128]{1,0:T(8,128)S(1)} %collective-permute-done.16, f32[2,8,128]{2,1,0:T(8,128)S(1)} %get-tuple-element.13), kind=kLoop, calls=%fused_computation.12 | loop fusion | flops 3072 | bytes 20480 | tf_op jit(solution)/shard_map/add | solution.py:128
  (12 shorter events, 0.0 us)
Async XLA Ops:
  0.0 0.8 %copy-start.1 = (bf16[8,32,128]{2,1,0:T(8,128)(2,1)S(1)}, bf16[8,32,128]{2,1,0:T(8,128)(2,1)}, u32[]{:S(2)}) copy-start(bf16[8,32,128]{2,1,0:T(8,128)(2,1)} %refs_0_) | copy-start | bytes 196612
  0.0 6.5 %copy-start.2 = (s32[128,8]{0,1:T(8,128)S(1)}, s32[128,8]{0,1:T(8,128)}, u32[]{:S(2)}) copy-start(s32[128,8]{0,1:T(8,128)} %param.7) | copy-start | bytes 12292
  0.0 6.5 %copy-start = (bf16[256,128,128]{2,1,0:T(8,128)(2,1)S(1)}, bf16[256,128,128]{2,1,0:T(8,128)(2,1)}, u32[]{:S(2)}) copy-start(bf16[256,128,128]{2,1,0:T(8,128)(2,1)} %refs_2_.3) | copy-start | bytes 25165828
  0.0 6.5 %copy-start.3 = (s32[256]{0:T(256)S(1)}, s32[256]{0:T(256)}, u32[]{:S(2)}) copy-start(s32[256]{0:T(256)} %lengths.9) | copy-start | bytes 3076
  0.8 5.6 %collective-permute-start = (bf16[8,32,128]{2,1,0:T(8,128)(2,1)S(1)}, bf16[8,32,128]{2,1,0:T(8,128)(2,1)S(1)}, u32[]{:S(2)}, u32[]{:S(2)}) collective-permute-start(bf16[8,32,128]{2,1,0:T(8,128)(2,1)S(1)} %copy-done.1), channel_id=1, source_target_pairs={{0,1},{1,0},{2,3},{3,2},{4,5},{5,4},{6,7},{7,6},{8,9},{9,8},{10,11... | collective-permute-start | bytes 196616 | tf_op jit(solution)/shard_map/ppermute | solution.py:101
  1.3 7.5 %collective-permute-start.1 = (bf16[8,32,128]{2,1,0:T(8,128)(2,1)S(1)}, bf16[8,32,128]{2,1,0:T(8,128)(2,1)S(1)}, u32[]{:S(2)}, u32[]{:S(2)}) collective-permute-start(bf16[8,32,128]{2,1,0:T(8,128)(2,1)S(1)} %copy-done.1), channel_id=1, source_target_pairs={{0,12},{1,13},{2,14},{3,15},{4,8},{5,9},{6,10},{7,11},{8,4},{9,5},... | collective-permute-start | bytes 196616 | tf_op jit(solution)/shard_map/ppermute | solution.py:101
  5.9 6.1 %collective-permute-start.6 = (bf16[8,32,128]{2,1,0:T(8,128)(2,1)S(1)}, bf16[8,32,128]{2,1,0:T(8,128)(2,1)S(1)}, u32[]{:S(2)}, u32[]{:S(2)}) collective-permute-start(bf16[8,32,128]{2,1,0:T(8,128)(2,1)S(1)} %copy-done.1), channel_id=1, source_target_pairs={{0,8},{1,9},{2,10},{3,11},{4,12},{5,13},{6,14},{7,15},{8,0},{9,1},... | collective-permute-start | bytes 196616 | tf_op jit(solution)/shard_map/ppermute | solution.py:101
  5.9 7.6 %collective-permute-start.11 = (bf16[8,32,128]{2,1,0:T(8,128)(2,1)S(1)}, bf16[8,32,128]{2,1,0:T(8,128)(2,1)S(1)}, u32[]{:S(2)}, u32[]{:S(2)}) collective-permute-start(bf16[8,32,128]{2,1,0:T(8,128)(2,1)S(1)} %copy-done.1), channel_id=1, source_target_pairs={{0,4},{1,5},{2,6},{3,7},{4,0},{5,1},{6,2},{7,3},{8,12},{9,13},{10,... | collective-permute-start | bytes 196616 | tf_op jit(solution)/shard_map/ppermute | solution.py:101
  8.8 5.2 %collective-permute-start.3 = (bf16[8,32,128]{2,1,0:T(8,128)(2,1)S(1)}, bf16[8,32,128]{2,1,0:T(8,128)(2,1)S(1)}, u32[]{:S(2)}, u32[]{:S(2)}) collective-permute-start(bf16[8,32,128]{2,1,0:T(8,128)(2,1)S(1)} %collective-permute-done.1.refs_0_), channel_id=1, source_target_pairs={{0,2},{1,3},{2,0},{3,1},{4,6},{5,7},{6,4},{7,5},{8,10},{9,11},{10,... | collective-permute-start | bytes 196616 | tf_op jit(solution)/shard_map/ppermute | solution.py:101
  10.4 4.7 %collective-permute-start.17 = (bf16[8,32,128]{2,1,0:T(8,128)(2,1)S(1)}, bf16[8,32,128]{2,1,0:T(8,128)(2,1)S(1)}, u32[]{:S(2)}, u32[]{:S(2)}) collective-permute-start(bf16[8,32,128]{2,1,0:T(8,128)(2,1)S(1)} %copy-done.1), channel_id=1, source_target_pairs={{0,2},{1,3},{2,0},{3,1},{4,6},{5,7},{6,4},{7,5},{8,10},{9,11},{10,... | collective-permute-start | bytes 196616 | tf_op jit(solution)/shard_map/ppermute | solution.py:101
  10.9 4.2 %collective-permute-start.2 = (bf16[8,32,128]{2,1,0:T(8,128)(2,1)S(1)}, bf16[8,32,128]{2,1,0:T(8,128)(2,1)S(1)}, u32[]{:S(2)}, u32[]{:S(2)}) collective-permute-start(bf16[8,32,128]{2,1,0:T(8,128)(2,1)S(1)} %collective-permute-done.1.refs_0_), channel_id=1, source_target_pairs={{0,1},{1,0},{2,3},{3,2},{4,5},{5,4},{6,7},{7,6},{8,9},{9,8},{10,11... | collective-permute-start | bytes 196616 | tf_op jit(solution)/shard_map/ppermute | solution.py:101
  12.0 5.0 %collective-permute-start.8 = (bf16[8,32,128]{2,1,0:T(8,128)(2,1)S(1)}, bf16[8,32,128]{2,1,0:T(8,128)(2,1)S(1)}, u32[]{:S(2)}, u32[]{:S(2)}) collective-permute-start(bf16[8,32,128]{2,1,0:T(8,128)(2,1)S(1)} %collective-permute-done.6.refs_0_), channel_id=1, source_target_pairs={{0,2},{1,3},{2,0},{3,1},{4,6},{5,7},{6,4},{7,5},{8,10},{9,11},{10,... | collective-permute-start | bytes 196616 | tf_op jit(solution)/shard_map/ppermute | solution.py:101
  13.5 4.3 %collective-permute-start.13 = (bf16[8,32,128]{2,1,0:T(8,128)(2,1)S(1)}, bf16[8,32,128]{2,1,0:T(8,128)(2,1)S(1)}, u32[]{:S(2)}, u32[]{:S(2)}) collective-permute-start(bf16[8,32,128]{2,1,0:T(8,128)(2,1)S(1)} %collective-permute-done.11.refs_0_), channel_id=1, source_target_pairs={{0,2},{1,3},{2,0},{3,1},{4,6},{5,7},{6,4},{7,5},{8,10},{9,11},{10,... | collective-permute-start | bytes 196616 | tf_op jit(solution)/shard_map/ppermute | solution.py:101
  14.1 3.8 %collective-permute-start.4 = (bf16[8,32,128]{2,1,0:T(8,128)(2,1)S(1)}, bf16[8,32,128]{2,1,0:T(8,128)(2,1)S(1)}, u32[]{:S(2)}, u32[]{:S(2)}) collective-permute-start(bf16[8,32,128]{2,1,0:T(8,128)(2,1)S(1)} %collective-permute-done.3.refs_2_), channel_id=1, source_target_pairs={{0,1},{1,0},{2,3},{3,2},{4,5},{5,4},{6,7},{7,6},{8,9},{9,8},{10,11... | collective-permute-start | bytes 196616 | tf_op jit(solution)/shard_map/ppermute | solution.py:101
  15.1 6.3 %collective-permute-start.7 = (bf16[8,32,128]{2,1,0:T(8,128)(2,1)S(1)}, bf16[8,32,128]{2,1,0:T(8,128)(2,1)S(1)}, u32[]{:S(2)}, u32[]{:S(2)}) collective-permute-start(bf16[8,32,128]{2,1,0:T(8,128)(2,1)S(1)} %collective-permute-done.6.refs_0_), channel_id=1, source_target_pairs={{0,1},{1,0},{2,3},{3,2},{4,5},{5,4},{6,7},{7,6},{8,9},{9,8},{10,11... | collective-permute-start | bytes 196616 | tf_op jit(solution)/shard_map/ppermute | solution.py:101
  15.1 13.3 %collective-permute-start.12 = (bf16[8,32,128]{2,1,0:T(8,128)(2,1)S(1)}, bf16[8,32,128]{2,1,0:T(8,128)(2,1)S(1)}, u32[]{:S(2)}, u32[]{:S(2)}) collective-permute-start(bf16[8,32,128]{2,1,0:T(8,128)(2,1)S(1)} %collective-permute-done.11.refs_0_), channel_id=1, source_target_pairs={{0,1},{1,0},{2,3},{3,2},{4,5},{5,4},{6,7},{7,6},{8,9},{9,8},{10,11... | collective-permute-start | bytes 196616 | tf_op jit(solution)/shard_map/ppermute | solution.py:101
  17.0 15.0 %collective-permute-start.18 = (bf16[8,32,128]{2,1,0:T(8,128)(2,1)S(1)}, bf16[8,32,128]{2,1,0:T(8,128)(2,1)S(1)}, u32[]{:S(2)}, u32[]{:S(2)}) collective-permute-start(bf16[8,32,128]{2,1,0:T(8,128)(2,1)S(1)} %collective-permute-done.17.refs_0_), channel_id=1, source_target_pairs={{0,1},{1,0},{2,3},{3,2},{4,5},{5,4},{6,7},{7,6},{8,9},{9,8},{10,11... | collective-permute-start | bytes 196616 | tf_op jit(solution)/shard_map/ppermute | solution.py:101
  17.8 7.1 %collective-permute-start.9 = (bf16[8,32,128]{2,1,0:T(8,128)(2,1)S(1)}, bf16[8,32,128]{2,1,0:T(8,128)(2,1)S(1)}, u32[]{:S(2)}, u32[]{:S(2)}) collective-permute-start(bf16[8,32,128]{2,1,0:T(8,128)(2,1)S(1)} %collective-permute-done.8.refs_2_), channel_id=1, source_target_pairs={{0,1},{1,0},{2,3},{3,2},{4,5},{5,4},{6,7},{7,6},{8,9},{9,8},{10,11... | collective-permute-start | bytes 196616 | tf_op jit(solution)/shard_map/ppermute | solution.py:101
  17.8 10.5 %collective-permute-start.14 = (bf16[8,32,128]{2,1,0:T(8,128)(2,1)S(1)}, bf16[8,32,128]{2,1,0:T(8,128)(2,1)S(1)}, u32[]{:S(2)}, u32[]{:S(2)}) collective-permute-start(bf16[8,32,128]{2,1,0:T(8,128)(2,1)S(1)} %collective-permute-done.13.refs_2_), channel_id=1, source_target_pairs={{0,1},{1,0},{2,3},{3,2},{4,5},{5,4},{6,7},{7,6},{8,9},{9,8},{10,11... | collective-permute-start | bytes 196616 | tf_op jit(solution)/shard_map/ppermute | solution.py:101
  21.4 12.6 %collective-permute-start.5 = (f32[4,8,128]{2,1,0:T(8,128)S(1)}, f32[4,8,128]{2,1,0:T(8,128)S(1)}, u32[]{:S(2)}, u32[]{:S(2)}) collective-permute-start(f32[4,8,128]{2,1,0:T(8,128)S(1)} %score.6), channel_id=1, source_target_pairs={{0,12},{1,13},{2,14},{3,15},{4,8},{5,9},{6,10},{7,11},{8,4},{9,5},... | collective-permute-start | bytes 49160 | tf_op jit(solution)/shard_map/ppermute | solution.py:101
  28.0 6.0 %collective-permute-start.10 = (f32[4,8,128]{2,1,0:T(8,128)S(1)}, f32[4,8,128]{2,1,0:T(8,128)S(1)}, u32[]{:S(2)}, u32[]{:S(2)}) collective-permute-start(f32[4,8,128]{2,1,0:T(8,128)S(1)} %score.7), channel_id=1, source_target_pairs={{0,8},{1,9},{2,10},{3,11},{4,12},{5,13},{6,14},{7,15},{8,0},{9,1},... | collective-permute-start | bytes 49160 | tf_op jit(solution)/shard_map/ppermute | solution.py:101
  31.4 3.7 %collective-permute-start.15 = (f32[4,8,128]{2,1,0:T(8,128)S(1)}, f32[4,8,128]{2,1,0:T(8,128)S(1)}, u32[]{:S(2)}, u32[]{:S(2)}) collective-permute-start(f32[4,8,128]{2,1,0:T(8,128)S(1)} %score.8), channel_id=1, source_target_pairs={{0,4},{1,5},{2,6},{3,7},{4,0},{5,1},{6,2},{7,3},{8,12},{9,13},{10,... | collective-permute-start | bytes 49160 | tf_op jit(solution)/shard_map/ppermute | solution.py:101
  35.2 3.7 %collective-permute-start.19 = (f32[8,128]{1,0:T(8,128)S(1)}, f32[8,128]{1,0:T(8,128)S(1)}, u32[]{:S(2)}, u32[]{:S(2)}) collective-permute-start(f32[8,128]{1,0:T(8,128)S(1)} %get-tuple-element.15), channel_id=1, source_target_pairs={{0,2},{1,3},{2,0},{3,1},{4,6},{5,7},{6,4},{7,5},{8,10},{9,11},{10,... | collective-permute-start | bytes 12296 | tf_op jit(solution)/shard_map/ppermute | solution.py:101
  36.1 3.0 %collective-permute-start.20 = (f32[8,128]{1,0:T(8,128)S(1)}, f32[8,128]{1,0:T(8,128)S(1)}, u32[]{:S(2)}, u32[]{:S(2)}) collective-permute-start(f32[8,128]{1,0:T(8,128)S(1)} %get-tuple-element.16), channel_id=1, source_target_pairs={{0,3},{1,2},{2,1},{3,0},{4,7},{5,6},{6,5},{7,4},{8,11},{9,10},{10,... | collective-permute-start | bytes 12296 | tf_op jit(solution)/shard_map/ppermute | solution.py:101
  36.1 3.0 %collective-permute-start.16 = (f32[8,128]{1,0:T(8,128)S(1)}, f32[8,128]{1,0:T(8,128)S(1)}, u32[]{:S(2)}, u32[]{:S(2)}) collective-permute-start(f32[8,128]{1,0:T(8,128)S(1)} %slice_bitcast_fusion.2), channel_id=1, source_target_pairs={{0,1},{1,0},{2,3},{3,2},{4,5},{5,4},{6,7},{7,6},{8,9},{9,8},{10,11... | collective-permute-start | bytes 12296 | tf_op jit(solution)/shard_map/ppermute | solution.py:101

commit v4 on v3

--- a/solution.py
+++ b/solution.py
@@ -30,10 +30,38 @@
     )()
 
 
-def score_kernel(shifts, n_blocks, candidates, lengths, own, *refs):
-    blocks, documents, out = refs[:n_blocks], refs[n_blocks], refs[n_blocks + 1]
+def table_kernel(candidates, lengths, table):
+    count = lengths.shape[0]
+    slots, lanes = table.shape[0], 128
+    for i in range(0, table.shape[1], lanes):
+        named = candidates[:, i : i + lanes]
+        row = jnp.maximum(named, 0)
+        length = jnp.zeros_like(row)
+        for j in range(0, count, lanes):
+            part = jnp.broadcast_to(lengths[j : j + lanes].reshape(1, lanes), (slots, lanes))
+            found = jnp.take_along_axis(part, row % lanes, axis=1)
+            length = jnp.where(row // lanes == j // lanes, found, length)
+        table[:, i : i + lanes] = row + jnp.where(named >= 0, length, 0) * (1 << count.bit_length())
+
+
+def table_of(candidates, lengths):
+    return pl.pallas_call(
+        table_kernel,
+        out_shape=jax.ShapeDtypeStruct(candidates.shape, candidates.dtype),
+        in_specs=[VMEM] * 2,
+        out_specs=VMEM,
+        compiler_params=pltpu.CompilerParams(vmem_limit_bytes=1 << 20),
+        name="table",
+    )(candidates, lengths)
+
+
+def score_kernel(shifts, n_blocks, n_known, table, own, *refs):
+    blocks, documents, outs = refs[:n_blocks], refs[n_blocks], refs[n_blocks + 1 :]
+    if n_known:
+        known, outs = outs[0], outs[1:]
     me = lax.axis_index("shard") * lax.axis_size("sub") + lax.axis_index("sub")
-    slots = candidates.shape[0]
+    slots = table.shape[0]
+    bits = documents.shape[0].bit_length()
     n_queries, terms, dim = blocks[0].shape
     tokens = documents.shape[1]
     group = dim // terms
@@ -41,6 +69,11 @@
     which = lax.broadcasted_iota(jnp.int32, (1, group * terms), 1) // terms
     member = lax.broadcasted_iota(jnp.int32, (group * terms, dim), 0) // terms
     mark = own[...]
+    per = n_blocks // len(outs)
+    fill = n_known // len(outs)
+    for i, out in enumerate(outs):
+        if n_known:
+            out[:fill] = known[i * fill : (i + 1) * fill]
 
     def group_scores(b, first):
         column = (me ^ shifts[b]) * n_queries + first
@@ -53,10 +86,9 @@
             sides = []
             limit = jnp.zeros((1, group * terms), jnp.int32)
             for g in range(group):
-                named = candidates[s, column + g]
-                place = jnp.maximum(named, 0)
-                sides.append(documents[place])
-                limit = jnp.where(which == g, jnp.where(named >= 0, lengths[place], 0), limit)
+                entry = table[s, column + g]
+                sides.append(documents[entry & ((1 << bits) - 1)])
+                limit = jnp.where(which == g, entry >> bits, limit)
             similar = lax.dot_general(
                 jnp.concatenate(sides, 1),
                 spread,
@@ -69,28 +101,31 @@
         for g in range(group):
             total = jnp.sum(jnp.where(which == g, top, 0.0), axis=1, keepdims=True)
             line = jnp.sum(mark * total, axis=0, keepdims=True)
-            out[b, first + g : first + g + 1, :] = line
+            outs[b // per][fill + b % per, first + g : first + g + 1, :] = line
 
     for b in range(n_blocks):
         for first in range(0, n_queries, group):
             group_scores(b, first)
 
 
-def score(shifts, candidates, lengths, own, blocks, documents):
+def score(shifts, table, own, blocks, documents, known=None, n_outs=1):
     n_blocks = len(blocks)
+    n_known = 0 if known is None else known.shape[0]
     n_queries, terms, dim = blocks[0].shape
     tokens = documents.shape[1]
-    pairs = n_blocks * n_queries * candidates.shape[0]
+    pairs = n_blocks * n_queries * table.shape[0]
     flops = 2 * pairs * terms * dim * tokens * 16
-    return pl.pallas_call(
-        functools.partial(score_kernel, shifts, n_blocks),
-        out_shape=jax.ShapeDtypeStruct((n_blocks, n_queries, own.shape[1]), jnp.float32),
-        in_specs=[SMEM] * 2 + [VMEM] * (n_blocks + 2),
-        out_specs=VMEM,
+    tile = ((n_blocks + n_known) // n_outs, n_queries, own.shape[1])
+    found = pl.pallas_call(
+        functools.partial(score_kernel, shifts, n_blocks, n_known),
+        out_shape=[jax.ShapeDtypeStruct(tile, jnp.float32)] * n_outs,
+        in_specs=[SMEM] + [VMEM] * (n_blocks + 2 + (n_known > 0)),
+        out_specs=[VMEM] * n_outs,
         compiler_params=pltpu.CompilerParams(vmem_limit_bytes=16 << 20),
         cost_estimate=pl.CostEstimate(flops=flops, bytes_accessed=0, transcendentals=0),
         name="score",
-    )(candidates, lengths, own, *blocks, documents)
+    )(table, own, *blocks, documents, *([known] if n_known else []))
+    return found if n_outs > 1 else found[0]
 
 
 def shards(queries, documents, doc_lengths, candidates):
@@ -103,25 +138,38 @@
     def after(value, *others):
         return lax.optimization_barrier((value, *others))[0]
 
-    columns = candidates.T
+    table = table_of(candidates.T, doc_lengths)
     own = lanes_of(candidates.shape[1], devices * candidates.shape[1])
     queries = after(queries, own)
     steps = [z * 4 for z in reversed(range(1, shard // 2))]
 
-    def scores(shifts, blocks):
-        return score(shifts, columns, doc_lengths, own, blocks, documents)
+    def scores(shifts, blocks, **more):
+        return score(shifts, table, own, blocks, documents, **more)
 
     along = {z: swap(queries, z) for z in steps}
-    beside = swap(queries, 2)
     near = scores((0, 1), [queries, swap(queries, 1)])
-    far = []
-    tied = {z: after(along[z], near) for z in steps}
-    across = {z: swap(tied[z], 2) for z in steps}
-    others = {z: swap(tied[z], 1) for z in steps}
+    beside = swap(after(queries, near), 2)
+    beyond = {}
+    parts = [steps[i : i + 3] for i in range(0, len(steps), 3)]
+    for i, z in enumerate(steps):
+        beyond[z] = swap(after(along[z], near), 2)
     back = []
-    for z in steps:
-        blocks = [along[z], others[z], across[z], swap(across[z], 1)]
-        back.append(swap(scores((z, z ^ 1, z ^ 2, z ^ 3), blocks), z))
+    for part in parts:
+        blocks, shifts = [], []
+        for z in part:
+            mine = after(along[z], near)
+            blocks += [mine, swap(mine, 1)]
+            shifts += [z, z ^ 1]
+        tiles = scores(tuple(shifts), blocks)
+        blocks, shifts = [], []
+        for z in part:
+            mine = after(beyond[z], tiles)
+            blocks += [mine, swap(mine, 1)]
+            shifts += [z ^ 2, z ^ 3]
+        found = scores(tuple(shifts), blocks, known=tiles, n_outs=len(part))
+        found = found if len(part) > 1 else [found]
+        back += [swap(f, z) for f, z in zip(found, part)]
+    beside = after(beside, found[0])
     far = scores((2, 3), [beside, swap(beside, 1)])
     near = sum((b[:2] for b in back), near)
     far = sum((b[2:] for b in back), far)

time: 39.9 us -> 37.6 us (0.942)
  waiting for transfers between devices: 7.75 us -> 6.39 us
  Pallas kernels: 13.1 us -> 12.3 us
    ppermute x21, waiting for transfers between devices: 7.75 us -> 6.39 us  [swap(): return lax.ppermute(value, AXES, [(i, i ^ k) for i in range(devices)])]
    pallas_call x5, Pallas kernels: 13.1 us -> 12.3 us  [the longest x4 12.2 us: score(): pl.pallas_call(functools.partial(score_kernel, shifts, n_blocks, n_known)...]
where the time goes in v4:
time: 37.6 us; the launch traced here: 37.5 us
  starting transfers between devices  17.2 us (46%)
  Pallas kernels  12.3 us (33%)
  waiting for transfers between devices  6.39 us (17%)
  local copies, waits for them, and re-layouts  0.83 us (2%)
  other arithmetic  0.61 us (2%)
    ppermute x21, starting transfers between devices, swap(): return lax.ppermute(value, AXES, [(i, i ^ k) for i in range(devices)])  17.2 us
    pallas_call x4, Pallas kernels, score(): pl.pallas_call(functools.partial(score_kernel, shifts, n_blocks, n_known)...  12.2 us
    ppermute x21, waiting for transfers between devices, swap(): return lax.ppermute(value, AXES, [(i, i ^ k) for i in range(devices)])  6.39 us
    unnamed x8, local copies, waits for them, and re-layouts  0.83 us
  transfers between devices with their start and end apart: 21, of which 8 were waited for; matrix products, arithmetic and copies ran while one was open for 0% of the time, Pallas kernels for 33%

profile of v4, /device:TPU:0, one launch (start us, length us, event | category | flops | bytes accessed | tf_op | source)
XLA Modules:
  0.0 37.5 jit_solution(13542265354229625455)
XLA Ops:
  0.0 0.8 %copy-done.1 = bf16[8,32,128]{2,1,0:T(8,128)(2,1)S(1)} copy-done((bf16[8,32,128]{2,1,0:T(8,128)(2,1)S(1)}, bf16[8,32,128]{2,1,0:T(8,128)(2,1)}, u32[]{:S(2)}) %copy-start.1) | copy-done | bytes 65560
  0.8 0.5 %collective-permute-start = (bf16[8,32,128]{2,1,0:T(8,128)(2,1)S(1)}, bf16[8,32,128]{2,1,0:T(8,128)(2,1)S(1)}, u32[]{:S(2)}, u32[]{:S(2)}) collective-permute-start(bf16[8,32,128]{2,1,0:T(8,128)(2,1)S(1)} %copy-done.1), channel_id=1, source_target_pairs={{0,1},{1,0},{2,3},{3,2},{4,5},{5,4},{6,7},{7,6},{8,9},{9,8},{10,11... | collective-permute-start | bytes 196616 | tf_op jit(solution)/shard_map/ppermute | solution.py:136
  1.3 3.6 %collective-permute-start.4 = (bf16[8,32,128]{2,1,0:T(8,128)(2,1)S(1)}, bf16[8,32,128]{2,1,0:T(8,128)(2,1)S(1)}, u32[]{:S(2)}, u32[]{:S(2)}) collective-permute-start(bf16[8,32,128]{2,1,0:T(8,128)(2,1)S(1)} %copy-done.1), channel_id=1, source_target_pairs={{0,8},{1,9},{2,10},{3,11},{4,12},{5,13},{6,14},{7,15},{8,0},{9,1},... | collective-permute-start | bytes 196616 | tf_op jit(solution)/shard_map/ppermute | solution.py:136
  4.9 1.6 %collective-permute-start.6 = (bf16[8,32,128]{2,1,0:T(8,128)(2,1)S(1)}, bf16[8,32,128]{2,1,0:T(8,128)(2,1)S(1)}, u32[]{:S(2)}, u32[]{:S(2)}) collective-permute-start(bf16[8,32,128]{2,1,0:T(8,128)(2,1)S(1)} %copy-done.1), channel_id=1, source_target_pairs={{0,4},{1,5},{2,6},{3,7},{4,0},{5,1},{6,2},{7,3},{8,12},{9,13},{10,... | collective-permute-start | bytes 196616 | tf_op jit(solution)/shard_map/ppermute | solution.py:136
  6.5 0.0 collective-permute-start.1
  6.5 0.1 table.1
  6.6 0.0 collective-permute-done.refs_1_
  6.6 2.0 %score.4 = f32[2,8,128]{2,1,0:T(8,128)S(1)} custom-call(s32[8,128]{1,0:T(8,128)S(1)} %table.1, f32[8,128]{1,0:T(8,128)S(1)} %lanes.1.own, bf16[8,32,128]{2,1,0:T(8,128)(2,1)S(1)} %copy-done.1, bf16[8,32,128]{2,1,0:T(8,128)(2,1)S(1)} %collective-permute-done.refs_1_, bf16[256,128,128]{2,1,0:T(8,128)(2,1)S(1)} %copy-done), custom_call_target="tpu_custom_call" | custom-call | flops 2147483648 | tf_op jit(solution)/shard_map/score/pallas_call | solution.py:119
  8.5 0.4 %collective-permute-done.4.refs_2_ = bf16[8,32,128]{2,1,0:T(8,128)(2,1)S(1)} collective-permute-done((bf16[8,32,128]{2,1,0:T(8,128)(2,1)S(1)}, bf16[8,32,128]{2,1,0:T(8,128)(2,1)S(1)}, u32[]{:S(2)}, u32[]{:S(2)}) %collective-permute-start.4) | collective-permute-done | bytes 65568 | tf_op jit(solution)/shard_map/ppermute | solution.py:136
  8.9 0.0 collective-permute-start.5
  9.0 0.4 %collective-permute-done.6.refs_4_ = bf16[8,32,128]{2,1,0:T(8,128)(2,1)S(1)} collective-permute-done((bf16[8,32,128]{2,1,0:T(8,128)(2,1)S(1)}, bf16[8,32,128]{2,1,0:T(8,128)(2,1)S(1)}, u32[]{:S(2)}, u32[]{:S(2)}) %collective-permute-start.6) | collective-permute-done | bytes 65568 | tf_op jit(solution)/shard_map/ppermute | solution.py:136
  9.4 0.1 collective-permute-start.7
  9.5 3.1 %collective-permute-done.1.refs_0_ = bf16[8,32,128]{2,1,0:T(8,128)(2,1)S(1)} collective-permute-done((bf16[8,32,128]{2,1,0:T(8,128)(2,1)S(1)}, bf16[8,32,128]{2,1,0:T(8,128)(2,1)S(1)}, u32[]{:S(2)}, u32[]{:S(2)}) %collective-permute-start.1) | collective-permute-done | bytes 65568 | tf_op jit(solution)/shard_map/ppermute | solution.py:136
  12.5 0.0 collective-permute-start.3
  12.5 1.5 %collective-permute-start.11 = (bf16[8,32,128]{2,1,0:T(8,128)(2,1)S(1)}, bf16[8,32,128]{2,1,0:T(8,128)(2,1)S(1)}, u32[]{:S(2)}, u32[]{:S(2)}) collective-permute-start(bf16[8,32,128]{2,1,0:T(8,128)(2,1)S(1)} %collective-permute-done.6.refs_4_), channel_id=1, source_target_pairs={{0,2},{1,3},{2,0},{3,1},{4,6},{5,7},{6,4},{7,5},{8,10},{9,11},{10,... | collective-permute-start | bytes 196616 | tf_op jit(solution)/shard_map/ppermute | solution.py:136
  14.0 0.5 %collective-permute-start.9 = (bf16[8,32,128]{2,1,0:T(8,128)(2,1)S(1)}, bf16[8,32,128]{2,1,0:T(8,128)(2,1)S(1)}, u32[]{:S(2)}, u32[]{:S(2)}) collective-permute-start(bf16[8,32,128]{2,1,0:T(8,128)(2,1)S(1)} %collective-permute-done.4.refs_2_), channel_id=1, source_target_pairs={{0,2},{1,3},{2,0},{3,1},{4,6},{5,7},{6,4},{7,5},{8,10},{9,11},{10,... | collective-permute-start | bytes 196616 | tf_op jit(solution)/shard_map/ppermute | solution.py:136
  14.6 0.0 collective-permute-done.5.refs_3_
  14.6 1.5 %collective-permute-start.2 = (bf16[8,32,128]{2,1,0:T(8,128)(2,1)S(1)}, bf16[8,32,128]{2,1,0:T(8,128)(2,1)S(1)}, u32[]{:S(2)}, u32[]{:S(2)}) collective-permute-start(bf16[8,32,128]{2,1,0:T(8,128)(2,1)S(1)} %collective-permute-done.1.refs_0_), channel_id=1, source_target_pairs={{0,2},{1,3},{2,0},{3,1},{4,6},{5,7},{6,4},{7,5},{8,10},{9,11},{10,... | collective-permute-start | bytes 196616 | tf_op jit(solution)/shard_map/ppermute | solution.py:136
  16.1 0.0 collective-permute-done.7.refs_5_
  16.1 0.0 collective-permute-done.3.refs_1_
  16.1 4.1 %score.5.refs_7_ = f32[6,8,128]{2,1,0:T(8,128)S(1)} custom-call(s32[8,128]{1,0:T(8,128)S(1)} %table.1, f32[8,128]{1,0:T(8,128)S(1)} %lanes.1.own, bf16[8,32,128]{2,1,0:T(8,128)(2,1)S(1)} %collective-permute-done.1.refs_0_, bf16[8,32,128]{2,1,0:T(8,128)(2,1)S(1)} %collective-permute-done.3.refs_1_, bf16[8,32,128]{2,1,0:T(8,128)(2,1)S(1)} %collective-permute-done.4.refs_2_, ...), custom_call_target="tpu_custom_call" | custom-call | flops 6442450944 | tf_op jit(solution)/shard_map/score/pallas_call | solution.py:119
  20.2 0.0 collective-permute-done.11.refs_4_
  20.2 0.1 collective-permute-start.12
  20.3 0.5 %collective-permute-start.10 = (bf16[8,32,128]{2,1,0:T(8,128)(2,1)S(1)}, bf16[8,32,128]{2,1,0:T(8,128)(2,1)S(1)}, u32[]{:S(2)}, u32[]{:S(2)}) collective-permute-start(bf16[8,32,128]{2,1,0:T(8,128)(2,1)S(1)} %collective-permute-done.9.refs_2_), channel_id=1, source_target_pairs={{0,1},{1,0},{2,3},{3,2},{4,5},{5,4},{6,7},{7,6},{8,9},{9,8},{10,11... | collective-permute-start | bytes 196616 | tf_op jit(solution)/shard_map/ppermute | solution.py:136
  20.8 0.0 collective-permute-done.2.refs_0_
  20.8 0.1 collective-permute-start.8
  20.9 0.5 %collective-permute-start.17 = (bf16[8,32,128]{2,1,0:T(8,128)(2,1)S(1)}, bf16[8,32,128]{2,1,0:T(8,128)(2,1)S(1)}, u32[]{:S(2)}, u32[]{:S(2)}) collective-permute-start(bf16[8,32,128]{2,1,0:T(8,128)(2,1)S(1)} %copy-done.1), channel_id=1, source_target_pairs={{0,2},{1,3},{2,0},{3,1},{4,6},{5,7},{6,4},{7,5},{8,10},{9,11},{10,... | collective-permute-start | bytes 196616 | tf_op jit(solution)/shard_map/ppermute | solution.py:136
  21.4 0.1 collective-permute-done.12.refs_5_
  21.6 0.2 collective-permute-done.10.refs_3_
  21.7 0.4 collective-permute-done.8.refs_1_
  22.1 4.2 %score.6 = (f32[4,8,128]{2,1,0:T(8,128)S(1)}, f32[4,8,128]{2,1,0:T(8,128)S(1)}, f32[4,8,128]{2,1,0:T(8,128)S(1)}) custom-call(s32[8,128]{1,0:T(8,128)S(1)} %table.1, f32[8,128]{1,0:T(8,128)S(1)} %lanes.1.own, bf16[8,32,128]{2,1,0:T(8,128)(2,1)S(1)} %collective-permute-done.2.refs_0_, bf16[8,32,128]{2,1,0:T(8,128)(2,1)S(1)} %collective-permute-done.8.refs_1_, ...), custom_call_target="tpu_custom_call" | custom-call | flops 6442450944 | tf_op jit(solution)/shard_map/score/pallas_call | solution.py:119
  26.2 0.0 collective-permute-done.17.refs_0_
  26.2 0.2 collective-permute-start.18
  26.5 1.6 %collective-permute-start.13 = (f32[4,8,128]{2,1,0:T(8,128)S(1)}, f32[4,8,128]{2,1,0:T(8,128)S(1)}, u32[]{:S(2)}, u32[]{:S(2)}) collective-permute-start(f32[4,8,128]{2,1,0:T(8,128)S(1)} %get-tuple-element.24), channel_id=1, source_target_pairs={{0,12},{1,13},{2,14},{3,15},{4,8},{5,9},{6,10},{7,11},{8,4},{9,5},... | collective-permute-start | bytes 49160 | tf_op jit(solution)/shard_map/ppermute | solution.py:136
  28.0 0.5 %collective-permute-start.14 = (f32[4,8,128]{2,1,0:T(8,128)S(1)}, f32[4,8,128]{2,1,0:T(8,128)S(1)}, u32[]{:S(2)}, u32[]{:S(2)}) collective-permute-start(f32[4,8,128]{2,1,0:T(8,128)S(1)} %get-tuple-element.25), channel_id=1, source_target_pairs={{0,8},{1,9},{2,10},{3,11},{4,12},{5,13},{6,14},{7,15},{8,0},{9,1},... | collective-permute-start | bytes 49160 | tf_op jit(solution)/shard_map/ppermute | solution.py:136
  28.5 2.3 %collective-permute-start.15 = (f32[4,8,128]{2,1,0:T(8,128)S(1)}, f32[4,8,128]{2,1,0:T(8,128)S(1)}, u32[]{:S(2)}, u32[]{:S(2)}) collective-permute-start(f32[4,8,128]{2,1,0:T(8,128)S(1)} %get-tuple-element.26), channel_id=1, source_target_pairs={{0,4},{1,5},{2,6},{3,7},{4,0},{5,1},{6,2},{7,3},{8,12},{9,13},{10,... | collective-permute-start | bytes 49160 | tf_op jit(solution)/shard_map/ppermute | solution.py:136
  30.9 0.0 collective-permute-done.18.refs_1_
  30.9 2.0 %score.7 = f32[2,8,128]{2,1,0:T(8,128)S(1)} custom-call(s32[8,128]{1,0:T(8,128)S(1)} %table.1, f32[8,128]{1,0:T(8,128)S(1)} %lanes.1.own, bf16[8,32,128]{2,1,0:T(8,128)(2,1)S(1)} %collective-permute-done.17.refs_0_, bf16[8,32,128]{2,1,0:T(8,128)(2,1)S(1)} %collective-permute-done.18.refs_1_, bf16[256,128,128]{2,1,0:T(8,128)(2,1)S(1)} %copy-done), custom_call_target="tpu_custom_call" | custom-call | flops 2147483648 | tf_op jit(solution)/shard_map/score/pallas_call | solution.py:119
  32.8 0.0 collective-permute-done.13
  32.8 0.0 collective-permute-done.14
  32.8 0.0 collective-permute-done.15
  32.9 1.0 %collective-permute-start.19 = (f32[8,128]{1,0:T(8,128)S(1)}, f32[8,128]{1,0:T(8,128)S(1)}, u32[]{:S(2)}, u32[]{:S(2)}) collective-permute-start(f32[8,128]{1,0:T(8,128)S(1)} %get-tuple-element.31), channel_id=1, source_target_pairs={{0,2},{1,3},{2,0},{3,1},{4,6},{5,7},{6,4},{7,5},{8,10},{9,11},{10,... | collective-permute-start | bytes 12296 | tf_op jit(solution)/shard_map/ppermute | solution.py:136
  33.8 0.0 collective-permute-start.20
  33.8 1.2 %collective-permute-start.16 = (f32[8,128]{1,0:T(8,128)S(1)}, f32[8,128]{1,0:T(8,128)S(1)}, u32[]{:S(2)}, u32[]{:S(2)}) collective-permute-start(f32[8,128]{1,0:T(8,128)S(1)} %slice_bitcast_fusion.2), channel_id=1, source_target_pairs={{0,1},{1,0},{2,3},{3,2},{4,5},{5,4},{6,7},{7,6},{8,9},{9,8},{10,11... | collective-permute-start | bytes 12296 | tf_op jit(solution)/shard_map/ppermute | solution.py:136
  35.1 1.5 %collective-permute-done.19 = f32[8,128]{1,0:T(8,128)S(1)} collective-permute-done((f32[8,128]{1,0:T(8,128)S(1)}, f32[8,128]{1,0:T(8,128)S(1)}, u32[]{:S(2)}, u32[]{:S(2)}) %collective-permute-start.19) | collective-permute-done | bytes 4128 | tf_op jit(solution)/shard_map/ppermute | solution.py:136
  36.5 0.3 collective-permute-done.20
  36.9 0.0 collective-permute-done.16
  36.9 0.6 %fusion.2 = f32[8,128]{1,0:T(8,128)} fusion(f32[8,128]{1,0:T(8,128)S(1)} %collective-permute-done.20, f32[8,128]{1,0:T(8,128)S(1)} %collective-permute-done.19, f32[8,128]{1,0:T(8,128)S(1)} %collective-permute-done.16, f32[2,8,128]{2,1,0:T(8,128)S(1)} %get-tuple-element.29), kind=kLoop, calls=%fused_computation.12 | loop fusion | flops 3072 | bytes 20480 | tf_op jit(solution)/shard_map/add | solution.py:176
  (12 shorter events, 0.0 us)
Async XLA Ops:
  0.0 0.8 %copy-start.1 = (bf16[8,32,128]{2,1,0:T(8,128)(2,1)S(1)}, bf16[8,32,128]{2,1,0:T(8,128)(2,1)}, u32[]{:S(2)}) copy-start(bf16[8,32,128]{2,1,0:T(8,128)(2,1)} %refs_0_) | copy-start | bytes 196612
  0.0 6.5 %copy-start.2 = (s32[128,8]{0,1:T(8,128)S(1)}, s32[128,8]{0,1:T(8,128)}, u32[]{:S(2)}) copy-start(s32[128,8]{0,1:T(8,128)} %param.7) | copy-start | bytes 12292
  0.0 6.5 %copy-start.3 = (s32[256]{0:T(256)S(1)}, s32[256]{0:T(256)}, u32[]{:S(2)}) copy-start(s32[256]{0:T(256)} %lengths.1) | copy-start | bytes 3076
  0.0 6.6 %copy-start = (bf16[256,128,128]{2,1,0:T(8,128)(2,1)S(1)}, bf16[256,128,128]{2,1,0:T(8,128)(2,1)}, u32[]{:S(2)}) copy-start(bf16[256,128,128]{2,1,0:T(8,128)(2,1)} %refs_2_.3) | copy-start | bytes 25165828
  0.8 5.7 %collective-permute-start = (bf16[8,32,128]{2,1,0:T(8,128)(2,1)S(1)}, bf16[8,32,128]{2,1,0:T(8,128)(2,1)S(1)}, u32[]{:S(2)}, u32[]{:S(2)}) collective-permute-start(bf16[8,32,128]{2,1,0:T(8,128)(2,1)S(1)} %copy-done.1), channel_id=1, source_target_pairs={{0,1},{1,0},{2,3},{3,2},{4,5},{5,4},{6,7},{7,6},{8,9},{9,8},{10,11... | collective-permute-start | bytes 196616 | tf_op jit(solution)/shard_map/ppermute | solution.py:136
  1.3 7.7 %collective-permute-start.4 = (bf16[8,32,128]{2,1,0:T(8,128)(2,1)S(1)}, bf16[8,32,128]{2,1,0:T(8,128)(2,1)S(1)}, u32[]{:S(2)}, u32[]{:S(2)}) collective-permute-start(bf16[8,32,128]{2,1,0:T(8,128)(2,1)S(1)} %copy-done.1), channel_id=1, source_target_pairs={{0,8},{1,9},{2,10},{3,11},{4,12},{5,13},{6,14},{7,15},{8,0},{9,1},... | collective-permute-start | bytes 196616 | tf_op jit(solution)/shard_map/ppermute | solution.py:136
  4.9 4.5 %collective-permute-start.6 = (bf16[8,32,128]{2,1,0:T(8,128)(2,1)S(1)}, bf16[8,32,128]{2,1,0:T(8,128)(2,1)S(1)}, u32[]{:S(2)}, u32[]{:S(2)}) collective-permute-start(bf16[8,32,128]{2,1,0:T(8,128)(2,1)S(1)} %copy-done.1), channel_id=1, source_target_pairs={{0,4},{1,5},{2,6},{3,7},{4,0},{5,1},{6,2},{7,3},{8,12},{9,13},{10,... | collective-permute-start | bytes 196616 | tf_op jit(solution)/shard_map/ppermute | solution.py:136
  6.5 6.1 %collective-permute-start.1 = (bf16[8,32,128]{2,1,0:T(8,128)(2,1)S(1)}, bf16[8,32,128]{2,1,0:T(8,128)(2,1)S(1)}, u32[]{:S(2)}, u32[]{:S(2)}) collective-permute-start(bf16[8,32,128]{2,1,0:T(8,128)(2,1)S(1)} %copy-done.1), channel_id=1, source_target_pairs={{0,12},{1,13},{2,14},{3,15},{4,8},{5,9},{6,10},{7,11},{8,4},{9,5},... | collective-permute-start | bytes 196616 | tf_op jit(solution)/shard_map/ppermute | solution.py:136
  8.9 5.6 %collective-permute-start.5 = (bf16[8,32,128]{2,1,0:T(8,128)(2,1)S(1)}, bf16[8,32,128]{2,1,0:T(8,128)(2,1)S(1)}, u32[]{:S(2)}, u32[]{:S(2)}) collective-permute-start(bf16[8,32,128]{2,1,0:T(8,128)(2,1)S(1)} %collective-permute-done.4.refs_2_), channel_id=1, source_target_pairs={{0,1},{1,0},{2,3},{3,2},{4,5},{5,4},{6,7},{7,6},{8,9},{9,8},{10,11... | collective-permute-start | bytes 196616 | tf_op jit(solution)/shard_map/ppermute | solution.py:136
  9.4 6.7 %collective-permute-start.7 = (bf16[8,32,128]{2,1,0:T(8,128)(2,1)S(1)}, bf16[8,32,128]{2,1,0:T(8,128)(2,1)S(1)}, u32[]{:S(2)}, u32[]{:S(2)}) collective-permute-start(bf16[8,32,128]{2,1,0:T(8,128)(2,1)S(1)} %collective-permute-done.6.refs_4_), channel_id=1, source_target_pairs={{0,1},{1,0},{2,3},{3,2},{4,5},{5,4},{6,7},{7,6},{8,9},{9,8},{10,11... | collective-permute-start | bytes 196616 | tf_op jit(solution)/shard_map/ppermute | solution.py:136
  12.5 3.6 %collective-permute-start.3 = (bf16[8,32,128]{2,1,0:T(8,128)(2,1)S(1)}, bf16[8,32,128]{2,1,0:T(8,128)(2,1)S(1)}, u32[]{:S(2)}, u32[]{:S(2)}) collective-permute-start(bf16[8,32,128]{2,1,0:T(8,128)(2,1)S(1)} %collective-permute-done.1.refs_0_), channel_id=1, source_target_pairs={{0,1},{1,0},{2,3},{3,2},{4,5},{5,4},{6,7},{7,6},{8,9},{9,8},{10,11... | collective-permute-start | bytes 196616 | tf_op jit(solution)/shard_map/ppermute | solution.py:136
  12.5 7.7 %collective-permute-start.11 = (bf16[8,32,128]{2,1,0:T(8,128)(2,1)S(1)}, bf16[8,32,128]{2,1,0:T(8,128)(2,1)S(1)}, u32[]{:S(2)}, u32[]{:S(2)}) collective-permute-start(bf16[8,32,128]{2,1,0:T(8,128)(2,1)S(1)} %collective-permute-done.6.refs_4_), channel_id=1, source_target_pairs={{0,2},{1,3},{2,0},{3,1},{4,6},{5,7},{6,4},{7,5},{8,10},{9,11},{10,... | collective-permute-start | bytes 196616 | tf_op jit(solution)/shard_map/ppermute | solution.py:136
  14.0 6.3 %collective-permute-start.9 = (bf16[8,32,128]{2,1,0:T(8,128)(2,1)S(1)}, bf16[8,32,128]{2,1,0:T(8,128)(2,1)S(1)}, u32[]{:S(2)}, u32[]{:S(2)}) collective-permute-start(bf16[8,32,128]{2,1,0:T(8,128)(2,1)S(1)} %collective-permute-done.4.refs_2_), channel_id=1, source_target_pairs={{0,2},{1,3},{2,0},{3,1},{4,6},{5,7},{6,4},{7,5},{8,10},{9,11},{10,... | collective-permute-start | bytes 196616 | tf_op jit(solution)/shard_map/ppermute | solution.py:136
  14.6 6.3 %collective-permute-start.2 = (bf16[8,32,128]{2,1,0:T(8,128)(2,1)S(1)}, bf16[8,32,128]{2,1,0:T(8,128)(2,1)S(1)}, u32[]{:S(2)}, u32[]{:S(2)}) collective-permute-start(bf16[8,32,128]{2,1,0:T(8,128)(2,1)S(1)} %collective-permute-done.1.refs_0_), channel_id=1, source_target_pairs={{0,2},{1,3},{2,0},{3,1},{4,6},{5,7},{6,4},{7,5},{8,10},{9,11},{10,... | collective-permute-start | bytes 196616 | tf_op jit(solution)/shard_map/ppermute | solution.py:136
  20.2 1.3 %collective-permute-start.12 = (bf16[8,32,128]{2,1,0:T(8,128)(2,1)S(1)}, bf16[8,32,128]{2,1,0:T(8,128)(2,1)S(1)}, u32[]{:S(2)}, u32[]{:S(2)}) collective-permute-start(bf16[8,32,128]{2,1,0:T(8,128)(2,1)S(1)} %collective-permute-done.11.refs_4_), channel_id=1, source_target_pairs={{0,1},{1,0},{2,3},{3,2},{4,5},{5,4},{6,7},{7,6},{8,9},{9,8},{10,11... | collective-permute-start | bytes 196616 | tf_op jit(solution)/shard_map/ppermute | solution.py:136
  20.3 1.4 %collective-permute-start.10 = (bf16[8,32,128]{2,1,0:T(8,128)(2,1)S(1)}, bf16[8,32,128]{2,1,0:T(8,128)(2,1)S(1)}, u32[]{:S(2)}, u32[]{:S(2)}) collective-permute-start(bf16[8,32,128]{2,1,0:T(8,128)(2,1)S(1)} %collective-permute-done.9.refs_2_), channel_id=1, source_target_pairs={{0,1},{1,0},{2,3},{3,2},{4,5},{5,4},{6,7},{7,6},{8,9},{9,8},{10,11... | collective-permute-start | bytes 196616 | tf_op jit(solution)/shard_map/ppermute | solution.py:136
  20.8 1.3 %collective-permute-start.8 = (bf16[8,32,128]{2,1,0:T(8,128)(2,1)S(1)}, bf16[8,32,128]{2,1,0:T(8,128)(2,1)S(1)}, u32[]{:S(2)}, u32[]{:S(2)}) collective-permute-start(bf16[8,32,128]{2,1,0:T(8,128)(2,1)S(1)} %collective-permute-done.2.refs_0_), channel_id=1, source_target_pairs={{0,1},{1,0},{2,3},{3,2},{4,5},{5,4},{6,7},{7,6},{8,9},{9,8},{10,11... | collective-permute-start | bytes 196616 | tf_op jit(solution)/shard_map/ppermute | solution.py:136
  20.9 5.3 %collective-permute-start.17 = (bf16[8,32,128]{2,1,0:T(8,128)(2,1)S(1)}, bf16[8,32,128]{2,1,0:T(8,128)(2,1)S(1)}, u32[]{:S(2)}, u32[]{:S(2)}) collective-permute-start(bf16[8,32,128]{2,1,0:T(8,128)(2,1)S(1)} %copy-done.1), channel_id=1, source_target_pairs={{0,2},{1,3},{2,0},{3,1},{4,6},{5,7},{6,4},{7,5},{8,10},{9,11},{10,... | collective-permute-start | bytes 196616 | tf_op jit(solution)/shard_map/ppermute | solution.py:136
  26.2 4.6 %collective-permute-start.18 = (bf16[8,32,128]{2,1,0:T(8,128)(2,1)S(1)}, bf16[8,32,128]{2,1,0:T(8,128)(2,1)S(1)}, u32[]{:S(2)}, u32[]{:S(2)}) collective-permute-start(bf16[8,32,128]{2,1,0:T(8,128)(2,1)S(1)} %collective-permute-done.17.refs_0_), channel_id=1, source_target_pairs={{0,1},{1,0},{2,3},{3,2},{4,5},{5,4},{6,7},{7,6},{8,9},{9,8},{10,11... | collective-permute-start | bytes 196616 | tf_op jit(solution)/shard_map/ppermute | solution.py:136
  26.5 6.4 %collective-permute-start.13 = (f32[4,8,128]{2,1,0:T(8,128)S(1)}, f32[4,8,128]{2,1,0:T(8,128)S(1)}, u32[]{:S(2)}, u32[]{:S(2)}) collective-permute-start(f32[4,8,128]{2,1,0:T(8,128)S(1)} %get-tuple-element.24), channel_id=1, source_target_pairs={{0,12},{1,13},{2,14},{3,15},{4,8},{5,9},{6,10},{7,11},{8,4},{9,5},... | collective-permute-start | bytes 49160 | tf_op jit(solution)/shard_map/ppermute | solution.py:136
  28.0 4.8 %collective-permute-start.14 = (f32[4,8,128]{2,1,0:T(8,128)S(1)}, f32[4,8,128]{2,1,0:T(8,128)S(1)}, u32[]{:S(2)}, u32[]{:S(2)}) collective-permute-start(f32[4,8,128]{2,1,0:T(8,128)S(1)} %get-tuple-element.25), channel_id=1, source_target_pairs={{0,8},{1,9},{2,10},{3,11},{4,12},{5,13},{6,14},{7,15},{8,0},{9,1},... | collective-permute-start | bytes 49160 | tf_op jit(solution)/shard_map/ppermute | solution.py:136
  28.5 4.3 %collective-permute-start.15 = (f32[4,8,128]{2,1,0:T(8,128)S(1)}, f32[4,8,128]{2,1,0:T(8,128)S(1)}, u32[]{:S(2)}, u32[]{:S(2)}) collective-permute-start(f32[4,8,128]{2,1,0:T(8,128)S(1)} %get-tuple-element.26), channel_id=1, source_target_pairs={{0,4},{1,5},{2,6},{3,7},{4,0},{5,1},{6,2},{7,3},{8,12},{9,13},{10,... | collective-permute-start | bytes 49160 | tf_op jit(solution)/shard_map/ppermute | solution.py:136
  32.9 3.7 %collective-permute-start.19 = (f32[8,128]{1,0:T(8,128)S(1)}, f32[8,128]{1,0:T(8,128)S(1)}, u32[]{:S(2)}, u32[]{:S(2)}) collective-permute-start(f32[8,128]{1,0:T(8,128)S(1)} %get-tuple-element.31), channel_id=1, source_target_pairs={{0,2},{1,3},{2,0},{3,1},{4,6},{5,7},{6,4},{7,5},{8,10},{9,11},{10,... | collective-permute-start | bytes 12296 | tf_op jit(solution)/shard_map/ppermute | solution.py:136
  33.8 3.0 %collective-permute-start.20 = (f32[8,128]{1,0:T(8,128)S(1)}, f32[8,128]{1,0:T(8,128)S(1)}, u32[]{:S(2)}, u32[]{:S(2)}) collective-permute-start(f32[8,128]{1,0:T(8,128)S(1)} %get-tuple-element.32), channel_id=1, source_target_pairs={{0,3},{1,2},{2,1},{3,0},{4,7},{5,6},{6,5},{7,4},{8,11},{9,10},{10,... | collective-permute-start | bytes 12296 | tf_op jit(solution)/shard_map/ppermute | solution.py:136
  33.8 3.0 %collective-permute-start.16 = (f32[8,128]{1,0:T(8,128)S(1)}, f32[8,128]{1,0:T(8,128)S(1)}, u32[]{:S(2)}, u32[]{:S(2)}) collective-permute-start(f32[8,128]{1,0:T(8,128)S(1)} %slice_bitcast_fusion.2), channel_id=1, source_target_pairs={{0,1},{1,0},{2,3},{3,2},{4,5},{5,4},{6,7},{7,6},{8,9},{9,8},{10,11... | collective-permute-start | bytes 12296 | tf_op jit(solution)/shard_map/ppermute | solution.py:136
